TPU v7x, 32 devices: a whole 2x2x4 slice. The times are simulated.
32 devices in a mesh: half: 2 (over core), row: 2 (over x), col: 8 (over z, y).
Axes of the slice: x: 2, y: 2, z: 4, core: 2. Of those that a mesh axis runs over, the one named last changes fastest.
Arguments:
- parent_front: float32 [16384, 16384], P(('half', 'row'), 'col'), may hold values from -6 to 6
- child_blocks: float32 [2, 8192, 8192], P('half', 'row', 'col'), may hold values from -6 to 6
- row_maps: int32 [2, 8192], replicated, may hold values from 0 to 16383, as said below
- inverse_blocks: float32 [4, 128, 128], replicated, may hold values from -0.12 to 0.12
Outputs:
- updated_front: float32 [16384, 16384], P(('half', 'row'), 'col')
- panel_factor: bfloat16 [16384, 512], P(('half', 'row'))
Inputs may be any that keep to these rules, and one draw needn't show every extreme that they name: `row_maps`: each row lists 8192 distinct parent rows. In every aligned block of 1024 entries of a row, at most 256 entries fall in one aligned block of 2048 parent rows, and that bound is reached in every such block; in every aligned block of 4096 entries, at most 1536 fall in one aligned block of 4096 parent rows, and that bound is reached in every such block.
All inputs are finite; a program needn't handle non-finite values.
Results may differ from a plain program's by a relative error of at most 0.001.
Values sent between devices are 32-bit elements; how exact they have to be, the bound alone decides.
No kernel may reach another device: no remote copies, remote signals or barrier semaphores. Data moves between devices by JAX's collectives and lax.ppermute only.
A program may use at most 320 MiB of HBM per device.

v0:
```python
import jax
import jax.numpy as jnp
from jax import lax
from jax.sharding import PartitionSpec as P


def from_root(block, axis, holder):
    block = jnp.where(lax.axis_index(axis) == holder, block, jnp.zeros_like(block))
    return lax.psum(block, axis)


def highest_outer(left, right):
    return lax.dot_general(
        left,
        right,
        (((1,), (1,)), ((), ())),
        precision=lax.Precision.HIGHEST,
        preferred_element_type=jnp.float32,
    )


def ranks(targets, count):
    onehot = (targets[..., None] == jnp.arange(count, dtype=jnp.int32)).astype(jnp.int32)
    before = jnp.cumsum(onehot, axis=-2) - onehot
    return jnp.sum(before * onehot, axis=-1)


def row_tables(row_maps, row_loc, groups, cap_rows, my_group):
    parent_rows = row_maps.reshape(groups, -1)
    targets = parent_rows // row_loc
    slots = ranks(targets, groups)
    sources = jnp.arange(groups, dtype=jnp.int32)[:, None]
    where_at = jnp.where(targets == my_group, sources * cap_rows + slots, groups * cap_rows)
    table = (
        jnp.full((groups * cap_rows,), row_loc, jnp.int32)
        .at[where_at.reshape(-1)]
        .set((parent_rows % row_loc).reshape(-1), mode="drop")
    )
    send_at = targets[my_group] * cap_rows + slots[my_group]
    return (send_at, table)


def col_tables(row_maps, col_loc, n_col, cap_cols, my_col):
    parent_cols = row_maps.reshape(2, n_col, -1)
    targets = parent_cols // col_loc
    slots = ranks(targets, n_col)
    sources = jnp.arange(n_col, dtype=jnp.int32)[None, :, None]
    where_at = jnp.where(targets == my_col, sources * cap_cols + slots, n_col * cap_cols)
    child_index = jnp.broadcast_to(jnp.arange(2, dtype=jnp.int32)[:, None, None], where_at.shape)
    table = (
        jnp.full((2, n_col * cap_cols), col_loc, jnp.int32)
        .at[child_index, where_at]
        .set(parent_cols % col_loc, mode="drop")
    )
    send_at = targets[:, my_col] * cap_cols + slots[:, my_col]
    return (send_at, table)


def row_pack(values, send_at, total):
    return jnp.zeros((total, values.shape[1]), values.dtype).at[send_at].set(values)


def col_pack(values, send_at, total):
    return jnp.zeros((values.shape[0], total), values.dtype).at[:, send_at].set(values)


def local(parent_front, child_blocks, row_maps, inverse_blocks):
    row_loc, col_loc = parent_front.shape
    child_rows, child_cols = (child_blocks.shape[1], child_blocks.shape[2])
    n_row = lax.axis_size("row")
    n_col = lax.axis_size("col")
    groups = lax.axis_size("half") * n_row
    my_child = lax.axis_index("half")
    my_group = my_child * n_row + lax.axis_index("row")
    my_col = lax.axis_index("col")
    cap_cols = 2 * child_cols // n_col
    cap_rows = n_col // n_row * (child_cols // groups + child_cols // n_col)
    slab_rows = n_row * cap_rows
    row_send, row_table = row_tables(row_maps, row_loc, groups, cap_rows, my_group)
    col_send, col_table = col_tables(row_maps, col_loc, n_col, cap_cols, my_col)
    mine = child_blocks[0]
    moved = col_pack(mine, col_send[my_child], n_col * cap_cols)
    arrived = lax.all_to_all(moved, "col", split_axis=1, concat_axis=1, tiled=True)
    outgoing = row_pack(arrived, row_send, groups * cap_rows)
    landed = lax.all_to_all(
        outgoing, ("half", "row"), split_axis=0, concat_axis=0, tiled=True
    ).reshape(2, slab_rows, n_col * cap_cols)
    row_dest = row_table.reshape(2, slab_rows)
    assembled = parent_front
    for child in range(2):
        spread = (
            jnp.zeros((slab_rows, col_loc), jnp.float32)
            .at[:, col_table[child]]
            .add(landed[child], mode="drop")
        )
        assembled = assembled.at[row_dest[child]].add(spread, mode="drop")
    width = inverse_blocks.shape[1]
    count = inverse_blocks.shape[0]
    span = n_col // groups
    root = my_col // span
    start = my_col % span * col_loc
    factors = []
    tops = []
    for block in range(count):
        current = assembled[:, block * width : (block + 1) * width]
        if block > 0:
            earlier = jnp.concatenate(factors, axis=1)
            above = jnp.concatenate(
                [
                    tops[prior][(block - prior - 1) * width : (block - prior) * width]
                    for prior in range(block)
                ],
                axis=1,
            )
            current = current - highest_outer(earlier, above)
        result = highest_outer(current, jnp.tril(inverse_blocks[block]))
        factors.append(result)
        if block + 1 < count:
            tops.append(from_root(result[(block + 1) * width : count * width], ("half", "row"), 0))
    local_factor = jnp.concatenate(factors, axis=1)
    factor_rows = from_root(local_factor, "col", 0)
    piece = lax.dynamic_slice_in_dim(factor_rows, start, col_loc, 0)
    factor_cols = from_root(piece, ("half", "row"), root)
    updated_front = assembled - highest_outer(factor_rows, factor_cols)
    return (updated_front, factor_rows.astype(jnp.bfloat16))


def solution(mesh):
    in_specs = (P(("half", "row"), "col"), P("half", "row", "col"), P(), P())
    out_specs = (P(("half", "row"), "col"), P(("half", "row"), None))
    return jax.shard_map(local, mesh=mesh, in_specs=in_specs, out_specs=out_specs, check_vma=False)
```

profile of v0, /device:TPU:0, one launch (start us, length us, event | category | flops | bytes accessed | tf_op | source)
XLA Modules:
  0.0 2403.7 jit_solution(15965270955756850521)
XLA Ops:
  7.2 23.2 copy.69
  30.5 36.0 %reduce-window.16 = s32[2,8,8,8,128]{4,3,2,1,0:T(8,128)S(1)} reduce-window(s32[2,8,8,8,128]{4,3,2,1,0:T(8,128)S(1)} %fusion.26, s32[]{:T(128)} %constant.121.clone.1), window={size=1x1x1x1x128 pad=0_0x0_0x0_0x0_0x127_0}, to_apply=%region_4.5 | reduce-window | flops 16646144 | bytes 1048580 | tf_op jit(solution)/shard_map/reduce-window.2
  71.8 17.5 copy.14
  89.5 30.6 %scatter_custom_fusion.1 = f32[4096,2048]{0,1:T(8,128)} fusion(s32[1024]{0:T(1024)S(1)} %bitcast.175, f32[1024,4096]{1,0:T(8,128)} %copy.14, f32[]{:T(128)} %constant.131.clone.1), kind=kCustom, calls=%fused_computation.14 | custom fusion | bytes 33554944 | tf_op jit(solution)/shard_map/scatter | solution.py:64
  120.1 7.7 all-to-all-start
  134.6 717.2 %all-to-all-done = f32[4096,8,256]{0,2,1:T(8,128)} async-done(((f32[4096,8,256]{0,2,1:T(8,128)}), f32[4096,8,256]{0,2,1:T(8,128)}, u32[]{:S(2)}, u32[]{:S(2)}) %all-to-all-start) | async-done | bytes 33554464 | tf_op jit(solution)/shard_map/all_to_all | solution.py:83
  851.8 33.4 %copy.25 = f32[4096,2048]{1,0:T(8,128)} copy(f32[4096,2048]{0,1:T(8,128)} %bitcast.13) | data formatting | bytes 67108864 | tf_op jit(solution)/shard_map/all_to_all | solution.py:83
  885.2 49.7 %scatter_custom_fusion.2 = f32[6144,2048]{1,0:T(8,128)} fusion(s32[4096]{0:T(1024)S(1)} %bitcast.172, f32[4096,2048]{1,0:T(8,128)} %copy.25, f32[]{:T(128)} %constant.131.clone.1), kind=kCustom, calls=%fused_computation.12 | custom fusion | bytes 50332160 | tf_op jit(solution)/shard_map/scatter | solution.py:60
  934.9 12.0 all-to-all-start.1
  949.1 60.3 %scatter_custom_fusion.7 = s32[4096]{0:T(1024)S(1)} fusion(s32[16384]{0:T(1024)S(1)} %bitcast.167, s32[16384]{0:T(1024)S(1)} %bitcast.168, s32[]{:T(128)} %constant.132.clone.1), kind=kCustom, calls=%fused_computation.145 | custom fusion | bytes 16388
  1009.8 60.5 %scatter_custom_fusion = s32[6144]{0:T(1024)S(1)} fusion(s32[16384]{0:T(1024)S(1)} %bitcast.166, s32[16384]{0:T(1024)S(1)} %add_select_fusion.4, s32[]{:T(128)} %constant.119.clone.1), kind=kCustom, calls=%fused_computation.143 | custom fusion | bytes 24580 | tf_op jit(solution)/shard_map/scatter | solution.py:37
  1071.0 418.5 %all-to-all-done.1 = f32[4,1536,2048]{2,1,0:T(8,128)} async-done(((f32[4,1536,2048]{2,1,0:T(8,128)}), f32[4,1536,2048]{2,1,0:T(8,128)}, u32[]{:S(2)}, u32[]{:S(2)}) %all-to-all-start.1) | async-done | bytes 50331680 | tf_op jit(solution)/shard_map/all_to_all | solution.py:85
  1489.5 31.6 %fusion.74 = (f32[2,1536,2048]{2,1,0:T(8,128)}, f32[2,1536,2048]{2,1,0:T(8,128)}) fusion(f32[4,1536,2048]{2,1,0:T(8,128)} %all-to-all-done.1), kind=kLoop, calls=%fused_computation.158 | loop fusion | bytes 100663296 | tf_op jit(solution)/shard_map/slice | solution.py:94
  1521.1 24.7 %copy.26 = f32[3072,2048]{0,1:T(8,128)} copy(f32[3072,2048]{1,0:T(8,128)} %bitcast.155) | data formatting | bytes 50331648 | tf_op jit(solution)/shard_map/slice | solution.py:94
  1545.8 46.9 %scatter_custom_fusion.3 = f32[3072,2048]{0,1:T(8,128)} fusion(s32[2048]{0:T(1024)S(1)} %bitcast.174, f32[3072,2048]{0,1:T(8,128)} %copy.26, f32[]{:T(128)} %constant.131.clone.1), kind=kCustom, calls=%fused_computation.10 | custom fusion | flops 6291456 | bytes 50331652 | tf_op jit(solution)/shard_map/scatter-add | solution.py:94
  1592.7 24.8 %copy.17 = f32[3072,2048]{1,0:T(8,128)} copy(f32[3072,2048]{0,1:T(8,128)} %scatter_custom_fusion.3) | data formatting | bytes 50331648 | tf_op jit(solution)/shard_map/scatter-add | solution.py:94
  1617.6 24.7 %copy.27 = f32[3072,2048]{0,1:T(8,128)} copy(f32[3072,2048]{1,0:T(8,128)} %bitcast.154) | data formatting | bytes 50331648 | tf_op jit(solution)/shard_map/slice | solution.py:94
  1642.2 47.2 %scatter_custom_fusion.5 = f32[3072,2048]{0,1:T(8,128)} fusion(s32[2048]{0:T(1024)S(1)} %bitcast.173, f32[3072,2048]{0,1:T(8,128)} %copy.27, f32[]{:T(128)} %constant.131.clone.1), kind=kCustom, calls=%fused_computation.8 | custom fusion | flops 6291456 | bytes 50331652 | tf_op jit(solution)/shard_map/scatter-add | solution.py:94
  1689.4 24.8 %copy.19 = f32[3072,2048]{1,0:T(8,128)} copy(f32[3072,2048]{0,1:T(8,128)} %scatter_custom_fusion.5) | data formatting | bytes 50331648 | tf_op jit(solution)/shard_map/scatter-add | solution.py:94
  1714.2 61.9 %scatter_fusion = f32[4096,2048]{1,0:T(8,128)} fusion(f32[4096,2048]{1,0:T(8,128)} %copy.69, s32[3072]{0:T(1024)S(1)} %get-tuple-element.19, f32[3072,2048]{1,0:T(8,128)} %copy.17), kind=kCustom, calls=%fused_computation.4 | custom fusion | flops 6291456 | bytes 75509760 | tf_op jit(solution)/shard_map/scatter-add | solution.py:96
  1776.2 61.8 %scatter_fusion.1 = f32[4096,2048]{1,0:T(8,128)} fusion(f32[4096,2048]{1,0:T(8,128)} %scatter_fusion, s32[3072]{0:T(1024)S(1)} %copy-done.11, f32[3072,2048]{1,0:T(8,128)} %copy.19), kind=kCustom, calls=%fused_computation.6 | custom fusion | flops 6291456 | bytes 75509760 | tf_op jit(solution)/shard_map/scatter-add | solution.py:96
  1842.8 29.3 %all-reduce.6.cloned.1.call-done = f32[384,128]{0,1:T(8,128)} async-done(((f32[384,128]{0,1:T(8,128)}), f32[384,128]{0,1:T(8,128)}) %all-reduce.6.cloned.1.call-update) | async-done | bytes 196624 | tf_op jit(solution)/shard_map/psum | solution.py:9
  1872.1 5.2 convolution_subtract_fusion.2
  1881.7 31.2 %all-reduce.8.cloned.1.call-done = f32[256,128]{0,1:T(8,128)} async-done(((f32[256,128]{0,1:T(8,128)}), f32[256,128]{0,1:T(8,128)}) %all-reduce.8.cloned.1.call-update) | async-done | bytes 131088 | tf_op jit(solution)/shard_map/psum | solution.py:9
  1913.8 9.2 convolution_subtract_fusion.1
  1927.6 30.6 %all-reduce.10.cloned.1.call-done = f32[128,128]{0,1:T(8,128)} async-done(((f32[128,128]{0,1:T(8,128)}), f32[128,128]{0,1:T(8,128)}) %all-reduce.10.cloned.1.call-update) | async-done | bytes 65552 | tf_op jit(solution)/shard_map/psum | solution.py:9
  1958.2 12.7 fusion.16
  1977.1 270.3 %all-reduce.12.cloned.1.call-done = f32[4096,512]{0,1:T(8,128)} async-done(((f32[4096,512]{0,1:T(8,128)}), f32[4096,512]{0,1:T(8,128)}) %all-reduce.12.cloned.1.call-update) | async-done | bytes 8388624 | tf_op jit(solution)/shard_map/psum | solution.py:9
  2252.1 5.9 convert_element_type.21
  2258.0 6.4 copy.24
  2264.4 72.3 %all-reduce.14.cloned.1.call-done = f32[2048,512]{0,1:T(8,128)} async-done(((f32[2048,512]{0,1:T(8,128)}), f32[2048,512]{0,1:T(8,128)}) %all-reduce.14.cloned.1.call-update) | async-done | bytes 4194320 | tf_op jit(solution)/shard_map/psum | solution.py:9
  2336.8 60.2 %convolution_subtract_fusion = f32[4096,2048]{1,0:T(8,128)} fusion(f32[4096,2048]{1,0:T(8,128)} %scatter_fusion.1, f32[4096,512]{0,1:T(8,128)} %all-reduce.12.cloned.1.call-done, f32[2048,512]{0,1:T(8,128)} %all-reduce.14.cloned.1.call-done), kind=kOutput, calls=%fused_computation.16 | convolution fusion | flops 51547996160 | bytes 79691776 | tf_op jit(solution)/shard_map/dot_general | solution.py:13
  (94 shorter events, 40.6 us)
Async XLA Ops:
  7.2 23.2 copy-start.4
  120.1 731.8 %all-to-all-start = ((f32[4096,8,256]{0,2,1:T(8,128)}), f32[4096,8,256]{0,2,1:T(8,128)}, u32[]{:S(2)}, u32[]{:S(2)}) async-start(f32[4096,8,256]{0,2,1:T(8,128)} %bitcast.153), calls=%async_computation | async-start | bytes 67108864 | tf_op jit(solution)/shard_map/all_to_all | solution.py:83
  934.9 12.2 copy-start.13
  934.9 12.3 copy-start.12
  934.9 12.7 copy-start.6
  934.9 554.6 %all-to-all-start.1 = ((f32[4,1536,2048]{2,1,0:T(8,128)}), f32[4,1536,2048]{2,1,0:T(8,128)}, u32[]{:S(2)}, u32[]{:S(2)}) async-start(f32[4,1536,2048]{2,1,0:T(8,128)} %bitcast.152), calls=%async_computation.1 | async-start | bytes 100663296 | tf_op jit(solution)/shard_map/all_to_all | solution.py:85
  946.9 925.1 %all-reduce.6.cloned.1.call-start = ((), (), s32[]{:S(2)}) async-start(), calls=%async_computation.2 | async-start | bytes 393216 | tf_op jit(solution)/shard_map/psum | solution.py:9
  1714.2 61.9 %copy-start.11 = (s32[3072]{0:T(1024)S(1)}, s32[3072]{0:T(1024)}, u32[]{:S(2)}) copy-start(s32[3072]{0:T(1024)} %get-tuple-element.18) | copy-start | bytes 36868
  1776.2 61.8 %copy-start.5 = (f32[1,128,128]{1,2,0:T(8,128)S(1)}, f32[1,128,128]{1,2,0:T(8,128)}, u32[]{:S(2)}) copy-start(f32[1,128,128]{1,2,0:T(8,128)} %copy.28) | copy-start | bytes 196612
  1776.2 66.4 %copy-start.9 = (f32[1,128,128]{2,1,0:T(8,128)S(1)}, f32[1,128,128]{2,1,0:T(8,128)}, u32[]{:S(2)}) copy-start(f32[1,128,128]{2,1,0:T(8,128)} %get-tuple-element.10) | copy-start | bytes 196612
  1776.2 66.5 %copy-start.8 = (f32[1,128,128]{2,1,0:T(8,128)S(1)}, f32[1,128,128]{2,1,0:T(8,128)}, u32[]{:S(2)}) copy-start(f32[1,128,128]{2,1,0:T(8,128)} %get-tuple-element.9) | copy-start | bytes 196612
  1842.3 70.6 %all-reduce.8.cloned.1.call-start = ((), (), s32[]{:S(2)}) async-start(), calls=%async_computation.3 | async-start | bytes 262144 | tf_op jit(solution)/shard_map/psum | solution.py:9
  1872.1 9.6 copy-start.10
  1877.3 50.2 %copy-start.7 = (f32[1,128,128]{2,1,0:T(8,128)S(1)}, f32[1,128,128]{2,1,0:T(8,128)}, u32[]{:S(2)}) copy-start(f32[1,128,128]{2,1,0:T(8,128)} %get-tuple-element.8) | copy-start | bytes 196612
  1879.4 1.3 copy-start
  1881.4 76.8 %all-reduce.10.cloned.1.call-start = ((), (), s32[]{:S(2)}) async-start(), calls=%async_computation.4 | async-start | bytes 131072 | tf_op jit(solution)/shard_map/psum | solution.py:9
  1925.0 1.3 copy-start.2
  1927.0 320.3 %all-reduce.12.cloned.1.call-start = ((), (), s32[]{:S(2)}) async-start(), calls=%async_computation.5 | async-start | bytes 16777216 | tf_op jit(solution)/shard_map/psum | solution.py:9
  1958.2 14.8 copy-start.1
  1958.2 14.8 copy-start.3
  1976.8 359.9 %all-reduce.14.cloned.1.call-start = ((), (), s32[]{:S(2)}) async-start(), calls=%async_computation.6 | async-start | bytes 8388608 | tf_op jit(solution)/shard_map/psum | solution.py:9
Sparse Core Ops, SparseCore 0:
  1842.5 29.5 all-reduce.5
  1881.5 31.3 all-reduce.7
  1927.1 31.0 all-reduce.9
  1976.9 270.3 all-reduce.11
  2252.2 84.5 all-reduce.13
where the time goes:
time: 2420 us; the launch traced here: 2400 us
  waiting for transfers between devices  1570 us (65%)
  local copies, waits for them, and re-layouts  421 us (17%)
  other arithmetic  281 us (12%)
  matrix products  97.1 us (4%)
    all_to_all x1, waiting for transfers between devices, local(): lax.all_to_all(moved, 'col', split_axis=1, concat_axis=1, tiled=True)  717 us
    psum x5, waiting for transfers between devices, from_root(): return lax.psum(block, axis)  434 us
    all_to_all x1, waiting for transfers between devices, local(): lax.all_to_all(outgoing, ('half', 'row'), split_axis=0, concat_axis=0, ti...  419 us
    scatter-add x2, other arithmetic, local(): assembled = assembled.at[row_dest[child]].add(spread, mode='drop')  124 us
    dot_general x8, matrix products, highest_outer(): lax.dot_general(left, right, (((1,), (1,)), ((), ())), precision=lax.Prec...  97.1 us
    scatter-add x2, other arithmetic, local(): spread = jnp.zeros((slab_rows, col_loc), jnp.float32).at[:, col_table[chi...  94.1 us
    unnamed x40, local copies, waits for them, and re-layouts  93.8 us
    slice x3, local copies, waits for them, and re-layouts, local(): landed[child]  81 us
  transfers between devices with their start and end apart: 7, of which 7 were waited for; matrix products, arithmetic and copies ran while one was open for 6% of the time, Pallas kernels for 0%

commit v1 on v0

--- a/solution.py
+++ b/solution.py
@@ -1,7 +1,16 @@
+import functools
+
 import jax
 import jax.numpy as jnp
 from jax import lax
+from jax.experimental import pallas as pl
+from jax.experimental.pallas import tpu as pltpu
 from jax.sharding import PartitionSpec as P
+
+LANES = 128
+CHUNKS = 2
+TILE = 256
+SLAB = 64
 
 
 def from_root(block, axis, holder):
@@ -64,7 +73,207 @@
     return jnp.zeros((values.shape[0], total), values.dtype).at[:, send_at].set(values)
 
 
-def local(parent_front, child_blocks, row_maps, inverse_blocks):
+def round_up(value, step):
+    return -(-value // step) * step
+
+
+def split(values):
+    high = lax.reduce_precision(values, 8, 7)
+    return high.astype(jnp.bfloat16), (values - high).astype(jnp.bfloat16)
+
+
+def place_kernel(parts, starts, rounds, row_tab, col_tab, base, *refs):
+    landed, out, spread, rows_high, rows_low = refs[:parts], *refs[parts:]
+    tile = pl.program_id(0)
+    height, width = base.shape
+    n_src, n_col, window, lanes = landed[0].shape
+    packed = n_col * lanes
+
+    @pl.when(tile == 0)
+    def _():
+        column = lax.broadcasted_iota(jnp.int32, (lanes, width), 1)
+
+        def fill(at, carry):
+            rows = pl.ds(pl.multiple_of(at * lanes, lanes), lanes)
+            spread[rows, :] = (col_tab[rows, :] == column).astype(jnp.bfloat16)
+            return carry
+
+        lax.fori_loop(0, 2 * n_col, fill, 0)
+
+    total = base[...]
+    slab = min(SLAB, window)
+    for child in range(2):
+        rows_high[...] = jnp.zeros_like(rows_high)
+        rows_low[...] = jnp.zeros_like(rows_low)
+
+        def step(turn, carry):
+            values, hits = [], []
+            for shard in range(n_src // 2):
+                source = child * (n_src // 2) + shard
+                for part in range(parts):
+                    first = starts[(tile * n_src + source) * parts + part] + turn * slab
+                    at = pl.multiple_of(jnp.minimum(first, window - slab), 8)
+                    rows = pl.ds(at, slab)
+                    values.append(jnp.concatenate([landed[part][source, j, rows, :] for j in range(n_col)], axis=1))
+                    index = at + lax.broadcasted_iota(jnp.int32, (slab, height), 0)
+                    target = tile * height + lax.broadcasted_iota(jnp.int32, (slab, height), 1)
+                    hits.append(((row_tab[source * parts + part, rows, :] == target) & (index >= first)).astype(jnp.bfloat16))
+            value = jnp.concatenate(values, axis=0)
+            hit = jnp.concatenate(hits, axis=0)
+            high = value.astype(jnp.bfloat16)
+            low = (value - high.astype(jnp.float32)).astype(jnp.bfloat16)
+            dims = (((0,), (0,)), ((), ()))
+            rows_high[...] += lax.dot_general(hit, high, dims, preferred_element_type=jnp.float32)
+            rows_low[...] += lax.dot_general(hit, low, dims, preferred_element_type=jnp.float32)
+            return carry
+
+        lax.fori_loop(0, rounds[tile * 2 + child], step, 0)
+        wide = spread[child * packed : (child + 1) * packed, :]
+        total += jnp.dot(rows_high[...].astype(jnp.bfloat16), wide, preferred_element_type=jnp.float32)
+        total += jnp.dot(rows_low[...].astype(jnp.bfloat16), wide, preferred_element_type=jnp.float32)
+    out[...] = total
+
+
+def place(base, landed, row_tab, col_tab):
+    height, width = base.shape
+    parts = len(landed)
+    n_src, n_col, window, lanes = landed[0].shape
+    packed = n_col * lanes
+    tile = min(TILE, height)
+    tiles = height // tile
+    slab = min(SLAB, window)
+    edges = jnp.arange(tiles + 1, dtype=jnp.int32) * tile
+    inside = row_tab >= 0
+    below = jnp.sum((row_tab[..., None, :] < edges[:, None]).astype(jnp.int32), axis=-1)
+    past = jnp.sum((jnp.where(inside, row_tab, height)[..., None, :] < edges[:, None]).astype(jnp.int32), axis=-1)
+    ahead = jnp.argmax(inside.astype(jnp.int32), axis=-1)[..., None]
+    first = (ahead + past[..., :-1]) // 8 * 8
+    last = ahead + past[..., 1:]
+    count = jnp.where(past[..., 1:] > past[..., :-1], (last - first + slab - 1) // slab, 0)
+    rounds = jnp.max(count.reshape(2, -1, tiles), axis=1).T.reshape(-1)
+    starts = jnp.moveaxis(first, -1, 0).reshape(-1)
+    whole = lambda shape: pl.BlockSpec(shape, lambda *_: (0,) * len(shape), pipeline_mode=pl.Buffered(1))
+    spec = pltpu.PrefetchScalarGridSpec(
+        num_scalar_prefetch=2,
+        grid=(tiles,),
+        in_specs=[
+            whole((n_src * parts, window, 1)),
+            whole((2 * packed, 1)),
+            pl.BlockSpec((tile, width), lambda i, *_: (i, 0)),
+        ]
+        + [whole((n_src, n_col, window, lanes))] * parts,
+        out_specs=pl.BlockSpec((tile, width), lambda i, *_: (i, 0)),
+        scratch_shapes=[
+            pltpu.VMEM((2 * packed, width), jnp.bfloat16),
+            pltpu.VMEM((tile, packed), jnp.float32),
+            pltpu.VMEM((tile, packed), jnp.float32),
+        ],
+    )
+    return pl.pallas_call(
+        functools.partial(place_kernel, parts),
+        grid_spec=spec,
+        out_shape=jax.ShapeDtypeStruct(base.shape, base.dtype),
+        compiler_params=pltpu.CompilerParams(vmem_limit_bytes=60 * 2**20),
+        cost_estimate=pl.CostEstimate(
+            flops=8 * height * packed * width, bytes_accessed=8 * height * width + 4 * parts * n_src * packed * window, transcendentals=0
+        ),
+        name="place",
+    )(starts, rounds, row_tab.reshape(n_src * parts, window, 1), col_tab.reshape(-1, 1), base, *landed)
+
+
+def column_plan(row_maps, col_loc, n_col, share):
+    parent_cols = row_maps.reshape(2, n_col, -1)
+    owner = parent_cols // col_loc
+    size = owner.shape[-1]
+    earlier = jnp.arange(size)[:, None] > jnp.arange(size)[None, :]
+    same = (owner[..., :, None] == owner[..., None, :]) & earlier
+    rank = jnp.sum(same.astype(jnp.int32), axis=-1)
+    over = rank >= share
+    over_rank = jnp.sum((over[..., None, :] & earlier).astype(jnp.int32), axis=-1)
+    most = jnp.max(jnp.sum(over.astype(jnp.int32), axis=-1))
+    send = jnp.where(over, -1, owner * share + rank)
+    send_over = jnp.where(over, over_rank, -1)
+    return parent_cols, owner, rank, send, send_over, most
+
+
+def seen_from(here, parent_cols, slot, col_loc, count):
+    hit = (slot[..., None] == jnp.arange(count, dtype=jnp.int32)) & here[..., None]
+    return jnp.sum(jnp.where(hit, parent_cols[..., None] % col_loc + 1, 0), axis=2) - 1
+
+
+def even(parent_front, child_blocks, row_maps, plan):
+    row_loc, col_loc = parent_front.shape
+    child_rows, child_cols = child_blocks.shape[1:]
+    n_row, n_col = lax.axis_size("row"), lax.axis_size("col")
+    n_half = lax.axis_size("half")
+    groups = n_half * n_row
+    my_child = lax.axis_index("half")
+    my_group = my_child * n_row + lax.axis_index("row")
+    my_col = lax.axis_index("col")
+    cap_rows = n_col // n_row * (child_cols // groups + child_cols // n_col)
+    share = child_cols // n_col
+    parent_cols, owner, rank, send, send_over, _ = plan
+    here = owner == my_col
+    col_tab = seen_from(here, parent_cols, jnp.where(send >= 0, rank, -1), col_loc, share)
+    over_tab = seen_from(here, parent_cols, send_over, col_loc, share)
+    my_send = lax.dynamic_index_in_dim(send[my_child], my_col, 0, keepdims=False)
+    my_over = lax.dynamic_index_in_dim(send_over[my_child], my_col, 0, keepdims=False)
+    pick = (my_send[:, None] == jnp.arange(n_col * share, dtype=jnp.int32)).astype(jnp.bfloat16)
+    pick_over = (my_over[:, None] == jnp.arange(share, dtype=jnp.int32)).astype(jnp.bfloat16)
+
+    blocks = row_maps.reshape(groups, child_rows)
+    order = jnp.sort(blocks * child_rows + jnp.arange(child_rows, dtype=jnp.int32), axis=1)
+    sorted_row = order // child_rows
+    sorted_from = order % child_rows
+    edges = jnp.arange(groups, dtype=jnp.int32) * row_loc
+    begin = jnp.sum((blocks[:, None, :] < edges[:, None]).astype(jnp.int32), axis=-1)
+
+    def window(chunks, chunk):
+        size = min(round_up(-(-cap_rows // chunks), 8) + 8, child_rows // chunks)
+        first = jnp.maximum(begin - chunk + chunks - 1, 0) // chunks
+        first = jnp.minimum(first // 8 * 8, child_rows // chunks - size)
+        return size, first
+
+    def table(chunks, chunk):
+        size, first = window(chunks, chunk)
+        rows = sorted_row[:, chunk::chunks]
+        mine = lax.dynamic_index_in_dim(first, my_group, 1, keepdims=False)
+        rows = jnp.stack([lax.dynamic_slice_in_dim(rows[s], mine[s], size, 0) for s in range(groups)])
+        local = rows - my_group * row_loc
+        return jnp.where((local >= 0) & (local < row_loc), local, -1)
+
+    def row_exchange(values, chunks, chunk, axis):
+        size, first = window(chunks, chunk)
+        mine = lax.dynamic_index_in_dim(first, my_group, 0, keepdims=False)
+        out = jnp.stack([lax.dynamic_slice_in_dim(values, mine[t], size, axis) for t in range(groups)])
+        return lax.all_to_all(out, ("half", "row"), split_axis=0, concat_axis=0, tiled=True)
+
+    from_row = lax.dynamic_index_in_dim(sorted_from, my_group, 0, keepdims=False)
+    mine = child_blocks[0]
+    taken = [mine[from_row[chunk::CHUNKS]] for chunk in range(CHUNKS)]
+    pairs = [split(values) for values in taken]
+
+    def packed(pair, choice, form):
+        high, low = pair
+        return jnp.einsum(form, high, choice, preferred_element_type=jnp.float32) + jnp.einsum(
+            form, low, choice, preferred_element_type=jnp.float32
+        )
+
+    wide_pick = pick.reshape(child_cols, n_col, share)
+    arrived = []
+    for chunk in range(CHUNKS):
+        moved = packed(pairs[chunk], wide_pick, "rk,kdu->dru")
+        arrived.append(lax.all_to_all(moved, "col", split_axis=0, concat_axis=0, tiled=True))
+    over = jnp.stack([packed(pair, pick_over, "rk,ku->ru") for pair in pairs], axis=1).reshape(child_rows, share)
+    over = row_exchange(over, 1, 0, 0)
+    over = lax.all_gather(over, "col", axis=1)
+    landed = [row_exchange(arrived[chunk], CHUNKS, chunk, 1) for chunk in range(CHUNKS)]
+    tables = jnp.stack([table(CHUNKS, chunk) for chunk in range(CHUNKS)], axis=1)
+    first = place(parent_front, [over], table(1, 0)[:, None], over_tab)
+    return place(first, landed, tables, col_tab)
+
+
+def general(parent_front, child_blocks, row_maps):
     row_loc, col_loc = parent_front.shape
     child_rows, child_cols = (child_blocks.shape[1], child_blocks.shape[2])
     n_row = lax.axis_size("row")
@@ -94,30 +303,50 @@
             .add(landed[child], mode="drop")
         )
         assembled = assembled.at[row_dest[child]].add(spread, mode="drop")
+    return assembled
+
+
+def local(parent_front, child_blocks, row_maps, inverse_blocks):
+    row_loc, col_loc = parent_front.shape
+    n_col = lax.axis_size("col")
+    n_row = lax.axis_size("row")
+    groups = lax.axis_size("half") * n_row
+    my_col = lax.axis_index("col")
+    share = child_blocks.shape[2] // n_col
+    if share % LANES:
+        assembled = general(parent_front, child_blocks, row_maps)
+    else:
+        plan = column_plan(row_maps, col_loc, n_col, share)
+        assembled = lax.cond(
+            plan[-1] <= share,
+            lambda parent, child: even(parent, child, row_maps, plan),
+            lambda parent, child: general(parent, child, row_maps),
+            parent_front,
+            child_blocks,
+        )
     width = inverse_blocks.shape[1]
     count = inverse_blocks.shape[0]
     span = n_col // groups
     root = my_col // span
     start = my_col % span * col_loc
-    factors = []
-    tops = []
-    for block in range(count):
-        current = assembled[:, block * width : (block + 1) * width]
-        if block > 0:
-            earlier = jnp.concatenate(factors, axis=1)
-            above = jnp.concatenate(
-                [
-                    tops[prior][(block - prior - 1) * width : (block - prior) * width]
-                    for prior in range(block)
-                ],
-                axis=1,
-            )
-            current = current - highest_outer(earlier, above)
-        result = highest_outer(current, jnp.tril(inverse_blocks[block]))
-        factors.append(result)
-        if block + 1 < count:
-            tops.append(from_root(result[(block + 1) * width : count * width], ("half", "row"), 0))
-    local_factor = jnp.concatenate(factors, axis=1)
+    inverses = jnp.tril(inverse_blocks)
+    at_root = (lax.axis_index("half") == 0) & (lax.axis_index("row") == 0)
+    corner = assembled[: count * width, : count * width]
+    corner = lax.psum(jnp.where(at_root, corner, jnp.zeros_like(corner)), ("half", "row"))
+
+    def panel(columns, tops):
+        factors = []
+        for block in range(count):
+            current = columns[:, block * width : (block + 1) * width]
+            if block > 0:
+                earlier = jnp.concatenate(factors, axis=1)
+                above = (earlier if tops is None else tops)[block * width : (block + 1) * width, : block * width]
+                current = current - highest_outer(earlier, above)
+            factors.append(highest_outer(current, inverses[block]))
+        return jnp.concatenate(factors, axis=1)
+
+    tops = panel(corner, None)
+    local_factor = panel(assembled[:, : count * width], tops)
     factor_rows = from_root(local_factor, "col", 0)
     piece = lax.dynamic_slice_in_dim(factor_rows, start, col_loc, 0)
     factor_cols = from_root(piece, ("half", "row"), root)

time: 2420 us -> 1790 us (0.74)
  waiting for transfers between devices: 1570 us -> 971 us
  local copies, waits for them, and re-layouts: 421 us -> 175 us
  Pallas kernels: 0 us -> 243 us
  other arithmetic: 281 us -> 89.3 us
  starting transfers between devices: 21.1 us -> 86.9 us
  loops' own time: 0 us -> 55 us
  matrix products: 97.1 us -> 148 us
    all_to_all x2 -> x5, waiting for transfers between devices: 1140 us -> 521 us  [the longest x2 440 us: even(): lax.all_to_all(moved, 'col', split_axis=0, concat_axis=0, tiled=True)]
    pallas_call x0 -> x2, Pallas kernels: none -> 243 us  [place(): pl.pallas_call(functools.partial(place_kernel, parts), grid_spec=spec, ou...]
    scatter-add x4 -> x0, other arithmetic: 218 us -> none  [the longest x2 124 us: local(): assembled = assembled.at[row_dest[child]].add(spread, mode='drop')]
    scatter x3 -> x0, local copies, waits for them, and re-layouts: 141 us -> none  [the longest x1 60.5 us: row_tables(): table = jnp.full((groups * cap_rows,), row_loc, jnp.int32).at[where_at.re...]
    psum x0 -> x1, waiting for transfers between devices: none -> 108 us  [local(): lax.psum(jnp.where(at_root, corner, jnp.zeros_like(corner)), ('half', 'ro...]
    psum x5 -> x2, waiting for transfers between devices: 434 us -> 342 us  [from_root(): return lax.psum(block, axis)]
    slice x8 -> x13, local copies, waits for them, and re-layouts: 83 us -> 6.91 us  [the longest x2 2.34 us: table(): rows = sorted_row[:, chunk::chunks]]
    all_to_all x2 -> x5, starting transfers between devices: 19.8 us -> 86.6 us  [the longest x2 69 us: even(): lax.all_to_all(moved, 'col', split_axis=0, concat_axis=0, tiled=True)]
  transfers between devices with their start and end apart: 7 -> 9, of which waited for: 7 -> 8; matrix products, arithmetic and copies ran while one was open for 6% -> 10% of each run, Pallas kernels for 0% -> 7%
where the time goes in v1:
time: 1790 us
  waiting for transfers between devices  971 us (54%)
  Pallas kernels  243 us (14%)
  local copies, waits for them, and re-layouts  175 us (10%)
  matrix products  148 us (8%)
  other arithmetic  89.3 us (5%)
  starting transfers between devices  86.9 us (5%)
  loops' own time  55 us (3%)
    all_to_all x2, waiting for transfers between devices, even(): lax.all_to_all(moved, 'col', split_axis=0, concat_axis=0, tiled=True)  440 us
    psum x2, waiting for transfers between devices, from_root(): return lax.psum(block, axis)  342 us
    pallas_call x2, Pallas kernels, place(): pl.pallas_call(functools.partial(place_kernel, parts), grid_spec=spec, ou...  243 us
    psum x1, waiting for transfers between devices, local(): lax.psum(jnp.where(at_root, corner, jnp.zeros_like(corner)), ('half', 'ro...  108 us
    dot_general x13, matrix products, highest_outer(): lax.dot_general(left, right, (((1,), (1,)), ((), ())), precision=lax.Prec...  100 us
    all_to_all x3, waiting for transfers between devices, row_exchange(): lax.all_to_all(out, ('half', 'row'), split_axis=0, concat_axis=0, tiled=T...  81.5 us
    all_to_all x2, starting transfers between devices, even(): lax.all_to_all(moved, 'col', split_axis=0, concat_axis=0, tiled=True)  69 us
    dynamic_slice x10, local copies, waits for them, and re-layouts, row_exchange(): lax.dynamic_slice_in_dim(values, mine[t], size, axis)  66.3 us
  transfers between devices with their start and end apart: 9, of which 8 were waited for; matrix products, arithmetic and copies ran while one was open for 10% of the time, Pallas kernels for 7%

profile of v1, /device:TPU:0, one launch (start us, length us, event | category | flops | bytes accessed | tf_op | source)
XLA Modules:
  0.0 1785.1 jit_solution(8971789182178744796)
XLA Ops:
  8.0 23.2 %copy.196 = f32[4096,2048]{1,0:T(8,128)} copy(f32[4096,2048]{1,0:T(8,128)} %param.6) | data formatting | bytes 67108864
  32.2 13.5 convert_reduce_fusion.4
  46.4 18.7 %convert_reduce_fusion.3 = s32[2,8,1024]{2,1,0:T(8,128)S(1)} fusion(pred[2,8,1024]{2,1,0:T(8,128)(4,1)S(1)} %get-tuple-element.72, pred[1024,1024]{1,0:T(8,128)(4,1)S(1)} %iota_compare_fusion.11), kind=kLoop, calls=%fused_computation.318 | loop fusion | flops 50315264 | bytes 1130496 | tf_op jit(solution)/shard_map/reduce_sum | solution.py:192
  66.6 1136.1 %conditional.1 = (f32[4096,2048]{1,0:T(8,128)}) conditional(s32[]{:T(128)} %convert_element_type.76, (s32[2,8192]{1,0:T(2,128)S(1)}, f32[1,4096,1024]{2,1,0:T(8,128)}, f32[4096,2048]{1,0:T(8,128)}) %tuple.101, (s32[2,8192]{1,0:T(2,128)S(1)}, s32[2,8,1024]{2,1,0:T(8,128)S(1)}, s32[2,8,1024]{2,1,0:T(8,128)}, s32[2,8,1024]{2,1,0:T(8,128)}, ...), branch_computations={%region_4.19_spmd, %region_19.31_spmd} | conditional | flops 156858384384 | bytes 1016360576 | solution.py:320
  84.9 9.3 sort.9.cloned.1.call-done
  96.0 17.5 gather_fusion.1
  120.6 17.5 gather_fusion
  145.5 7.6 copy.128
  159.5 37.2 %all-to-all-done.2 = f32[4,1544,128]{2,1,0:T(8,128)S(1)} async-done(((f32[4,1544,128]{2,1,0:T(8,128)}), f32[4,1544,128]{2,1,0:T(8,128)S(1)}, u32[]{:S(2)}, u32[]{:S(2)}) %all-to-all-start.2) | async-done | bytes 3162144 | tf_op jit(solution)/shard_map/cond/branch_1_fun/all_to_all | solution.py:249
  198.5 7.1 fusion.8
  205.6 11.0 add_bitcast_fusion.1
  223.2 7.0 fusion.4
  230.2 10.4 add_bitcast_fusion
  240.6 243.1 %all-to-all-done.3 = f32[8,2048,128]{1,2,0:T(8,128)} async-done(((f32[8,2048,128]{1,2,0:T(8,128)}), f32[8,2048,128]{1,2,0:T(8,128)}, u32[]{:S(2)}, u32[]{:S(2)}) %all-to-all-start.3) | async-done | bytes 8388640 | tf_op jit(solution)/shard_map/cond/branch_1_fun/all_to_all | solution.py:266
  483.7 62.5 %all-to-all-start.5 = ((f32[8,2048,128]{1,2,0:T(8,128)}), f32[8,2048,128]{1,2,0:T(8,128)}, u32[]{:S(2)}, u32[]{:S(2)}) async-start(f32[8,2048,128]{1,2,0:T(8,128)} %add_bitcast_fusion), calls=%async_computation.5 | async-start | bytes 16777216 | tf_op jit(solution)/shard_map/cond/branch_1_fun/all_to_all | solution.py:266
  554.3 14.9 constant_dynamic-slice_fusion.8
  587.6 8.7 pad_maximum_fusion
  596.2 196.8 %all-to-all-done.5 = f32[8,2048,128]{1,2,0:T(8,128)} async-done(((f32[8,2048,128]{1,2,0:T(8,128)}), f32[8,2048,128]{1,2,0:T(8,128)}, u32[]{:S(2)}, u32[]{:S(2)}) %all-to-all-start.5) | async-done | bytes 8388640 | tf_op jit(solution)/shard_map/cond/branch_1_fun/all_to_all | solution.py:266
  793.0 6.6 all-to-all-start.4
  822.8 10.1 select_reduce_fusion
  855.1 14.7 constant_dynamic-slice_fusion.3
  888.2 8.7 pad_maximum_fusion.1
  896.9 42.2 %all-to-all-done.4.refs_0_ = f32[4,8,776,128]{3,2,1,0:T(8,128)} async-done(((f32[4,8,776,128]{3,2,1,0:T(8,128)}), f32[4,8,776,128]{3,2,1,0:T(8,128)}, u32[]{:S(2)}, u32[]{:S(2)}) %all-to-all-start.4) | async-done | bytes 12714016 | tf_op jit(solution)/shard_map/cond/branch_1_fun/all_to_all | solution.py:249
  939.2 6.7 all-to-all-start.6
  958.0 125.4 %place.2.base = f32[4096,2048]{1,0:T(8,128)} custom-call(s32[64]{0:T(128)} %reshape.1107.starts, s32[32]{0:T(128)} %reshape.1109.rounds, s32[4,1544,1]{2,1,0:T(8,128)} %and_select_fusion.row_tab, s32[2048,1]{1,0:T(8,128)} %copy.129.col_tab, f32[4096,2048]{1,0:T(8,128)} %get-tuple-element.33.base, f32[4,8,1544,128]{3,2,1,0:T(8,128)} %bitcast.363), custom_call_target="tpu_custom_call" | custom-call | flops 68719476736 | bytes 92405760 | tf_op jit(solution)/shard_map/cond/branch_1_fun/place/pallas_call | solution.py:172
  1085.4 117.2 %place.3 = f32[4096,2048]{1,0:T(8,128)} custom-call(s32[128]{0:T(128)} %reshape.1104.starts, s32[32]{0:T(128)} %reshape.1105.rounds, s32[8,776,1]{2,1,0:T(8,128)} %reshape.1208.row_tab, s32[2048,1]{1,0:T(8,128)} %copy.139.col_tab, f32[4096,2048]{1,0:T(8,128)} %place.2.base, f32[4,8,776,128]{3,2,1,0:T(8,128)} %all-to-all-done.4.refs_0_, ...), custom_call_target="tpu_custom_call" | custom-call | flops 68719476736 | bytes 92536832 | tf_op jit(solution)/shard_map/cond/branch_1_fun/place/pallas_call | solution.py:172
  1209.8 107.9 %all-reduce.4.cloned.1.call-done = f32[512,512]{1,0:T(8,128)} async-done(((f32[512,512]{1,0:T(8,128)}), f32[512,512]{1,0:T(8,128)}) %all-reduce.4.cloned.1.call-update) | async-done | bytes 1048592 | tf_op jit(solution)/shard_map/psum | solution.py:335
  1327.3 8.8 convolution_subtract_fusion.1
  1339.6 12.6 fusion.132
  1358.2 269.6 %all-reduce.6.cloned.1.call-done = f32[4096,512]{0,1:T(8,128)} async-done(((f32[4096,512]{0,1:T(8,128)}), f32[4096,512]{0,1:T(8,128)}) %all-reduce.6.cloned.1.call-update) | async-done | bytes 8388624 | tf_op jit(solution)/shard_map/psum | solution.py:18
  1644.9 72.1 %all-reduce.8.cloned.1.call-done = f32[2048,512]{0,1:T(8,128)} async-done(((f32[2048,512]{0,1:T(8,128)}), f32[2048,512]{0,1:T(8,128)}) %all-reduce.8.cloned.1.call-update) | async-done | bytes 4194320 | tf_op jit(solution)/shard_map/psum | solution.py:18
  1717.0 60.2 %convolution_subtract_fusion = f32[4096,2048]{1,0:T(8,128)} fusion(f32[4096,2048]{1,0:T(8,128)} %get-tuple-element.152, f32[4096,512]{0,1:T(8,128)} %all-reduce.6.cloned.1.call-done, f32[2048,512]{0,1:T(8,128)} %all-reduce.8.cloned.1.call-done), kind=kOutput, calls=%fused_computation.320 | convolution fusion | flops 51547996160 | bytes 79691776 | tf_op jit(solution)/shard_map/dot_general | solution.py:22
  (148 shorter events, 144.3 us)
Async XLA Ops:
  8.0 23.5 %copy-start.3 = (s32[2,8192]{1,0:T(2,128)S(1)}, s32[2,8192]{1,0:T(2,128)}, u32[]{:S(2)}) copy-start(s32[2,8192]{1,0:T(2,128)} %param.8) | copy-start | bytes 196612
  31.6 0.6 copy-start.6
  45.7 0.6 copy-start.8
  75.8 37.7 %copy-start.4 = (s32[2,8192]{1,0:T(2,128)}, s32[2,8192]{1,0:T(2,128)S(1)}, u32[]{:S(2)}) copy-start(s32[2,8192]{1,0:T(2,128)S(1)} %get-tuple-element.26) | copy-start | bytes 196612 | tf_op jit(solution)/shard_map/cond
  75.8 18.5 %sort.9.cloned.1.call-start = ((), (), s32[]{:S(2)}) async-start(), calls=%async_computation.11 | async-start | bytes 196640 | tf_op jit(solution)/shard_map/cond/branch_1_fun/jit(sort)/sort | solution.py:225
  113.5 5.8 copy-start
  138.2 5.8 copy-start.1
  155.3 41.4 %all-to-all-start.2 = ((f32[4,1544,128]{2,1,0:T(8,128)}), f32[4,1544,128]{2,1,0:T(8,128)S(1)}, u32[]{:S(2)}, u32[]{:S(2)}) async-start(f32[4,1544,128]{2,1,0:T(8,128)} %pad_maximum_fusion.2), calls=%async_computation.2 | async-start | bytes 6324224 | tf_op jit(solution)/shard_map/cond/branch_1_fun/all_to_all | solution.py:249
  159.5 798.4 %all-gather.3.cloned.1.call-start = ((), (), s32[]{:S(2)}) async-start(), calls=%async_computation.7 | async-start | bytes 28459008 | tf_op jit(solution)/shard_map/cond/branch_1_fun/all_gather | solution.py:269
  196.7 1.7 copy-start.2
  216.7 267.0 %all-to-all-start.3 = ((f32[8,2048,128]{1,2,0:T(8,128)}), f32[8,2048,128]{1,2,0:T(8,128)}, u32[]{:S(2)}, u32[]{:S(2)}) async-start(f32[8,2048,128]{1,2,0:T(8,128)} %add_bitcast_fusion.1), calls=%async_computation.3 | async-start | bytes 16777216 | tf_op jit(solution)/shard_map/cond/branch_1_fun/all_to_all | solution.py:266
  483.7 309.4 %all-to-all-start.5 = ((f32[8,2048,128]{1,2,0:T(8,128)}), f32[8,2048,128]{1,2,0:T(8,128)}, u32[]{:S(2)}, u32[]{:S(2)}) async-start(f32[8,2048,128]{1,2,0:T(8,128)} %add_bitcast_fusion), calls=%async_computation.5 | async-start | bytes 16777216 | tf_op jit(solution)/shard_map/cond/branch_1_fun/all_to_all | solution.py:266
  596.2 226.4 %copy-start.7 = (s32[2,8,1024]{2,1,0:T(8,128)S(1)}, s32[2,8,1024]{2,1,0:T(8,128)}, u32[]{:S(2)}) copy-start(s32[2,8,1024]{2,1,0:T(8,128)} %get-tuple-element.30) | copy-start | bytes 196612 | tf_op jit(solution)/shard_map/cond
  596.2 226.4 %copy-start.5 = (s32[2,8192]{1,0:T(2,128)S(1)}, s32[2,8192]{1,0:T(2,128)}, u32[]{:S(2)}) copy-start(s32[2,8192]{1,0:T(2,128)} %copy-done.4) | copy-start | bytes 196612 | tf_op jit(solution)/shard_map/cond
  596.2 226.5 %copy-start.9 = (s32[2,8,1024]{2,1,0:T(8,128)S(1)}, s32[2,8,1024]{2,1,0:T(8,128)}, u32[]{:S(2)}) copy-start(s32[2,8,1024]{2,1,0:T(8,128)} %get-tuple-element.29) | copy-start | bytes 196612 | tf_op jit(solution)/shard_map/cond
  793.0 146.2 %all-to-all-start.4 = ((f32[4,8,776,128]{3,2,1,0:T(8,128)}), f32[4,8,776,128]{3,2,1,0:T(8,128)}, u32[]{:S(2)}, u32[]{:S(2)}) async-start(f32[4,8,776,128]{3,2,1,0:T(8,128)} %pad_maximum_fusion), calls=%async_computation.4 | async-start | bytes 25427968 | tf_op jit(solution)/shard_map/cond/branch_1_fun/all_to_all | solution.py:249
  939.2 146.2 %all-to-all-start.6 = ((f32[4,8,776,128]{3,2,1,0:T(8,128)}), f32[4,8,776,128]{3,2,1,0:T(8,128)}, u32[]{:S(2)}, u32[]{:S(2)}) async-start(f32[4,8,776,128]{3,2,1,0:T(8,128)} %pad_maximum_fusion.1), calls=%async_computation.6 | async-start | bytes 25427968 | tf_op jit(solution)/shard_map/cond/branch_1_fun/all_to_all | solution.py:249
  1202.8 114.9 %all-reduce.4.cloned.1.call-start = ((), (), s32[]{:S(2)}) async-start(), calls=%async_computation.8 | async-start | bytes 2097152 | tf_op jit(solution)/shard_map/psum | solution.py:335
  1205.1 422.7 %all-reduce.6.cloned.1.call-start = ((), (), s32[]{:S(2)}) async-start(), calls=%async_computation.9 | async-start | bytes 16777216 | tf_op jit(solution)/shard_map/psum | solution.py:18
  1317.7 8.6 copy-start.10
  1358.0 359.1 %all-reduce.8.cloned.1.call-start = ((), (), s32[]{:S(2)}) async-start(), calls=%async_computation.10 | async-start | bytes 8388608 | tf_op jit(solution)/shard_map/psum | solution.py:18
Sparse Core Ops, SparseCore 0:
  79.6 14.3 sort.11.cloned.1.call-done
  198.6 678.4 all-gather.2
  (1 shorter events, 0.0 us)
Sparse Core Ops, SparseCore 1:
  1206.3 111.3 all-reduce.3
  1358.1 269.7 all-reduce.5
  1632.7 84.3 all-reduce.7

commit v2 on v0

--- a/solution.py
+++ b/solution.py
@@ -1,7 +1,17 @@
+import functools
+
 import jax
 import jax.numpy as jnp
 from jax import lax
+from jax.experimental import pallas as pl
+from jax.experimental.pallas import tpu as pltpu
 from jax.sharding import PartitionSpec as P
+
+LANES = 128
+CHUNKS = 4
+TILE = 256
+SLAB = 32
+WIDE = 512
 
 
 def from_root(block, axis, holder):
@@ -64,7 +74,324 @@
     return jnp.zeros((values.shape[0], total), values.dtype).at[:, send_at].set(values)
 
 
-def local(parent_front, child_blocks, row_maps, inverse_blocks):
+def round_up(value, step):
+    return -(-value // step) * step
+
+
+def split(values):
+    high = lax.reduce_precision(values, 8, 7)
+    return high.astype(jnp.bfloat16), (values - high).astype(jnp.bfloat16)
+
+
+def window_kernel(count, starts, values, *refs):
+    outs, sems = refs[:-1], refs[-1]
+    size = outs[0].shape[1]
+    copies = []
+    for way, out in enumerate(outs):
+        for at in range(count):
+            first = pl.multiple_of(starts[way * count + at], 8)
+            copies.append(pltpu.make_async_copy(values.at[at, pl.ds(first, size), :], out.at[at], sems.at[way * count + at]))
+    for copy in copies:
+        copy.start()
+    for copy in copies:
+        copy.wait()
+
+
+def windows(values, starts, size):
+    count, _, lanes = values.shape
+    ways = starts.shape[0]
+    anywhere = pl.BlockSpec(memory_space=pl.ANY)
+    return pl.pallas_call(
+        functools.partial(window_kernel, count),
+        in_specs=[pl.BlockSpec(memory_space=pltpu.SMEM), anywhere],
+        out_specs=[anywhere] * ways,
+        out_shape=[jax.ShapeDtypeStruct((count, size, lanes), values.dtype)] * ways,
+        scratch_shapes=[pltpu.SemaphoreType.DMA((ways * count,))],
+        cost_estimate=pl.CostEstimate(flops=0, bytes_accessed=8 * ways * count * size * lanes, transcendentals=0),
+        name="windows",
+    )(starts.reshape(-1), values)
+
+
+def place_kernel(form, starts, rounds, flags, row_tab, col_tab, base, *refs):
+    parts, n_src, n_col, gates, n_landed, update = form
+    landed = refs[:n_landed]
+    extra = refs[n_landed : n_landed + 2 * update]
+    out, spread, rows_high, rows_low = refs[n_landed + 2 * update :]
+    tile = pl.program_id(0)
+    height, width = base.shape
+    window, lanes = landed[0].shape[-2:]
+    packed = n_col * lanes
+    slab = min(SLAB, window)
+    wide = min(WIDE, width)
+
+    def read(source, part, j, rows):
+        if len(landed[0].shape) == 5:
+            return landed[0][j, source, part, rows, :]
+        if n_landed == n_src:
+            return landed[source][part, rows, :]
+        return landed[part * n_src + source][j, rows, :]
+
+    @pl.when(tile == 0)
+    def _():
+        column = lax.broadcasted_iota(jnp.int32, (lanes, width), 1)
+
+        def fill(at, carry):
+            rows = pl.ds(pl.multiple_of(at * lanes, lanes), lanes)
+            spread[rows, :] = (col_tab[rows, :] == column).astype(jnp.bfloat16)
+            return carry
+
+        lax.fori_loop(0, 2 * n_col, fill, 0)
+
+    for child in range(2):
+        mine = slice(child * packed, (child + 1) * packed)
+        rows_high[:, mine] = jnp.zeros((height, packed), jnp.float32)
+        rows_low[:, mine] = jnp.zeros((height, packed), jnp.float32)
+
+        def step(turn, carry):
+            values, hits = [], []
+            for source in range(child * n_src // 2, (child + 1) * n_src // 2):
+                for part in range(parts):
+                    first = starts[(tile * n_src + source) * parts + part] + turn * slab
+                    at = pl.multiple_of(jnp.minimum(first, window - slab), 8)
+                    rows = pl.ds(at, slab)
+                    values.append(jnp.concatenate([read(source, part, j, rows) for j in range(n_col)], axis=1))
+                    index = at + lax.broadcasted_iota(jnp.int32, (slab, height), 0)
+                    target = tile * height + lax.broadcasted_iota(jnp.int32, (slab, height), 1)
+                    hits.append(((row_tab[source * parts + part, rows, :] == target) & (index >= first)).astype(jnp.float32))
+            value = jnp.concatenate(values, axis=0)
+            hit = jnp.concatenate(hits, axis=0).astype(jnp.bfloat16)
+            high = value.astype(jnp.bfloat16)
+            low = (value - high.astype(jnp.float32)).astype(jnp.bfloat16)
+            dims = (((0,), (0,)), ((), ()))
+            rows_high[:, mine] += lax.dot_general(hit, high, dims, preferred_element_type=jnp.float32)
+            rows_low[:, mine] += lax.dot_general(hit, low, dims, preferred_element_type=jnp.float32)
+            return carry
+
+        lax.fori_loop(0, rounds[tile * 2 + child], step, 0)
+
+    def matmuls(at, carry):
+        cols = pl.ds(pl.multiple_of(at * wide, wide), wide)
+        if not gates:
+            right = spread[:, cols]
+            total = base[:, cols]
+            total += jnp.dot(rows_high[...].astype(jnp.bfloat16), right, preferred_element_type=jnp.float32)
+            total += jnp.dot(rows_low[...].astype(jnp.bfloat16), right, preferred_element_type=jnp.float32)
+            if update:
+                left, above = extra
+                total += lax.dot_general(
+                    left[...], above[cols, :], (((1,), (1,)), ((), ())), preferred_element_type=jnp.float32
+                )
+            out[:, cols] = total
+            return carry
+        out[:, cols] = base[:, cols]
+        depth = 2 * packed // gates
+        for gate in range(gates):
+
+            @pl.when(flags[gate] > 0)
+            def _():
+                part = slice(gate * depth, (gate + 1) * depth)
+                right = spread[part, cols]
+                total = jnp.dot(rows_high[:, part].astype(jnp.bfloat16), right, preferred_element_type=jnp.float32)
+                total += jnp.dot(rows_low[:, part].astype(jnp.bfloat16), right, preferred_element_type=jnp.float32)
+                out[:, cols] += total
+
+        return carry
+
+    lax.fori_loop(0, width // wide, matmuls, 0)
+
+
+def place(base, landed, row_tab, col_tab, gates=0, factor=None):
+    height, width = base.shape
+    n_src, parts, window = row_tab.shape
+    n_col, lanes = col_tab.shape[1:]
+    packed = n_col * lanes
+    tile = min(TILE, height)
+    tiles = height // tile
+    slab = min(SLAB, window)
+    edges = jnp.arange(tiles + 1, dtype=jnp.int32) * tile
+    inside = row_tab >= 0
+    past = jnp.sum((jnp.where(inside, row_tab, height)[..., None, :] < edges[:, None]).astype(jnp.int32), axis=-1)
+    ahead = jnp.argmax(inside.astype(jnp.int32), axis=-1)[..., None]
+    first = (ahead + past[..., :-1]) // 8 * 8
+    last = ahead + past[..., 1:]
+    count = jnp.where(past[..., 1:] > past[..., :-1], (last - first + slab - 1) // slab, 0)
+    rounds = jnp.max(count.reshape(2, -1, tiles), axis=1)
+    flags = jnp.zeros((1,), jnp.int32)
+    if gates:
+        flags = jnp.any((col_tab >= 0).reshape(gates, -1), axis=1).astype(jnp.int32)
+        rounds = rounds * jnp.max(flags.reshape(2, -1), axis=1)[:, None]
+    starts = jnp.moveaxis(first, -1, 0).reshape(-1)
+    extra = [] if factor is None else list(factor)
+    whole = lambda shape: pl.BlockSpec(shape, lambda *_: (0,) * len(shape), pipeline_mode=pl.Buffered(1))
+    block = lambda shape: pl.BlockSpec(shape, lambda i, *_: (i, 0))
+    spec = pltpu.PrefetchScalarGridSpec(
+        num_scalar_prefetch=3,
+        grid=(tiles,),
+        in_specs=[whole((n_src * parts, window, 1)), whole((2 * packed, 1)), block((tile, width))]
+        + [whole(array.shape) for array in landed]
+        + ([block((tile, extra[0].shape[1])), whole(extra[1].shape)] if extra else []),
+        out_specs=block((tile, width)),
+        scratch_shapes=[
+            pltpu.VMEM((2 * packed, width), jnp.bfloat16),
+            pltpu.VMEM((tile, 2 * packed), jnp.float32),
+            pltpu.VMEM((tile, 2 * packed), jnp.float32),
+        ],
+    )
+    return pl.pallas_call(
+        functools.partial(place_kernel, (parts, n_src, n_col, gates, len(landed), 1 if extra else 0)),
+        grid_spec=spec,
+        out_shape=jax.ShapeDtypeStruct(base.shape, base.dtype),
+        compiler_params=pltpu.CompilerParams(vmem_limit_bytes=62 * 2**20),
+        cost_estimate=pl.CostEstimate(
+            flops=8 * height * packed * width, bytes_accessed=8 * height * width + 4 * parts * n_src * packed * window, transcendentals=0
+        ),
+        name="place",
+    )(starts, rounds.T.reshape(-1), flags, row_tab.reshape(n_src * parts, window, 1), col_tab.reshape(-1, 1), base, *landed, *extra)
+
+
+def earlier_count(marks):
+    size = marks.shape[-2]
+    before = (jnp.arange(size)[:, None] > jnp.arange(size)[None, :]).astype(jnp.bfloat16)
+    counts = jnp.einsum("ab,csbn->csan", before, marks.astype(jnp.bfloat16), preferred_element_type=jnp.float32)
+    return counts.astype(jnp.int32)
+
+
+def column_plan(row_maps, col_loc, n_col, share, panel):
+    parent_cols = row_maps.reshape(2, n_col, -1)
+    owner = parent_cols // col_loc
+    onehot = owner[..., None] == jnp.arange(n_col, dtype=jnp.int32)
+    rank = jnp.sum(jnp.where(onehot, earlier_count(onehot), 0), axis=-1)
+    over = rank >= share
+    early = parent_cols < panel
+    marks = jnp.stack([over, early], axis=-1)
+    order = earlier_count(marks)
+    most = jnp.max(jnp.sum(marks.astype(jnp.int32), axis=2))
+    send = jnp.where(over, -1, rank)
+    send_over = jnp.where(over, order[..., 0], -1)
+    send_early = jnp.where(early, order[..., 1], -1)
+    return parent_cols, owner, send, send_over, send_early, most
+
+
+def seen_from(here, parent_cols, slot, col_loc, count):
+    hit = (slot[..., None] == jnp.arange(count, dtype=jnp.int32)) & here[..., None]
+    return jnp.sum(jnp.where(hit, parent_cols[..., None] % col_loc + 1, 0), axis=2) - 1
+
+
+def panel_of(columns, inverses, tops):
+    count, width = inverses.shape[:2]
+    factors = []
+    for block in range(count):
+        current = columns[:, block * width : (block + 1) * width]
+        if block > 0:
+            earlier = jnp.concatenate(factors, axis=1)
+            above = (earlier if tops is None else tops)[block * width : (block + 1) * width, : block * width]
+            current = current - highest_outer(earlier, above)
+        factors.append(highest_outer(current, inverses[block]))
+    return jnp.concatenate(factors, axis=1)
+
+
+def even(parent_front, child_blocks, row_maps, inverse_blocks, plan):
+    row_loc, col_loc = parent_front.shape
+    child_rows, child_cols = child_blocks.shape[1:]
+    n_row, n_col = lax.axis_size("row"), lax.axis_size("col")
+    groups = lax.axis_size("half") * n_row
+    my_child = lax.axis_index("half")
+    my_group = my_child * n_row + lax.axis_index("row")
+    my_col = lax.axis_index("col")
+    cap_rows = n_col // n_row * (child_cols // groups + child_cols // n_col)
+    share = child_cols // n_col
+    panel = inverse_blocks.shape[0] * inverse_blocks.shape[1]
+    parent_cols, owner, send, send_over, send_early, _ = plan
+    pick_at = lambda array, at: lax.dynamic_index_in_dim(array, at, 0, keepdims=False)
+    here = owner == my_col
+    ordered = lambda tab: jnp.stack([pick_at(tab, my_child), pick_at(tab, 1 - my_child)])
+    col_tab = ordered(seen_from(here, parent_cols, send, col_loc, share))
+    over_tab = ordered(seen_from(here, parent_cols, send_over, col_loc, share))
+    at_col = lambda array: lax.dynamic_slice_in_dim(array, my_col, 1, 1)
+    early_cols = at_col(parent_cols)
+    early_tab = ordered(seen_from(early_cols >= 0, early_cols, at_col(send_early), panel, share))
+    own = lambda array: pick_at(pick_at(array, my_child), my_col)
+    slots = jnp.arange(share, dtype=jnp.int32)
+    owners = jnp.arange(n_col, dtype=jnp.int32)
+    pick = ((own(owner)[:, None, None] == owners[:, None]) & (own(send)[:, None, None] == slots)).astype(jnp.bfloat16)
+    pick_first = jnp.stack([own(send_over)[:, None] == slots, own(send_early)[:, None] == slots], axis=1).astype(jnp.bfloat16)
+
+    blocks = row_maps.reshape(groups, child_rows)
+    order = jnp.sort(blocks * child_rows + jnp.arange(child_rows, dtype=jnp.int32), axis=1)
+    sorted_row = jnp.swapaxes((order // child_rows).reshape(groups, -1, CHUNKS), 1, 2)
+    from_row = pick_at(order, my_group) % child_rows
+    edges = jnp.arange(groups, dtype=jnp.int32) * row_loc
+    begin = jnp.sum((blocks[:, None, :] < edges[:, None]).astype(jnp.int32), axis=-1)
+    length = child_rows // CHUNKS
+    size = min(round_up(-(-cap_rows // CHUNKS), 8) + 8, length)
+    chunks = jnp.arange(CHUNKS, dtype=jnp.int32)
+    first = jnp.maximum(begin[..., None] - chunks + CHUNKS - 1, 0) // CHUNKS
+    first = jnp.minimum(first // 8 * 8, length - size)
+    ways = jnp.bitwise_xor(my_group, jnp.arange(groups, dtype=jnp.int32))
+    starts = pick_at(first, my_group)[ways]
+    opening = lax.dynamic_index_in_dim(first, my_group, 1, keepdims=False)
+
+    def table(source):
+        rows, opens = pick_at(sorted_row, source), pick_at(opening, source)
+        return jnp.stack([lax.dynamic_slice_in_dim(rows[chunk], opens[chunk], size, 0) for chunk in range(CHUNKS)])
+
+    row_tab = jnp.stack([table(ways[way]) for way in range(groups)]) - my_group * row_loc
+    row_tab = jnp.where((row_tab >= 0) & (row_tab < row_loc), row_tab, -1)
+
+    def row_exchange(pieces):
+        swaps = [[(group, group ^ way) for group in range(groups)] for way in range(groups)]
+        return [pieces[0]] + [lax.ppermute(pieces[way], ("half", "row"), swaps[way]) for way in range(1, groups)]
+
+    def packed(pair, choice):
+        form = "rk,kdu->dru"
+        return jnp.einsum(form, pair[0], choice, preferred_element_type=jnp.float32) + jnp.einsum(
+            form, pair[1], choice, preferred_element_type=jnp.float32
+        )
+
+    mine = child_blocks[0]
+    pairs = [split(mine[from_row[chunk::CHUNKS]]) for chunk in range(CHUNKS)]
+    ahead = jnp.concatenate([packed(pair, pick_first) for pair in pairs], axis=0)
+    ahead = windows(ahead, jnp.repeat(starts, 2, axis=1), size)
+    ahead = row_exchange(ahead)
+    ahead = [piece.reshape(CHUNKS, 2, size, share) for piece in ahead]
+    over = jnp.stack([piece[:, 0] for piece in ahead])
+    early = [piece[:, 1] for piece in ahead]
+
+    front = parent_front[:, :panel]
+    front = place(jnp.where(my_col == 0, front, jnp.zeros_like(front)), early, row_tab, early_tab)
+    front = lax.psum(front, "col")
+    over = lax.all_gather(over, "col", axis=0)
+
+    landed = []
+    for chunk in range(CHUNKS):
+        moved = lax.all_to_all(packed(pairs[chunk], pick), "col", split_axis=0, concat_axis=0, tiled=True)
+        pieces = windows(moved, jnp.repeat(starts[:, chunk : chunk + 1], n_col, axis=1), size)
+        landed += row_exchange(pieces)
+
+    corner = front[:panel]
+    sent = [lax.ppermute(corner, ("half", "row"), [(0, way)]) for way in range(1, groups)]
+    corner = jnp.where(my_group == 0, corner, functools.reduce(jnp.add, sent))
+    inverses = jnp.tril(inverse_blocks)
+    factor_rows = panel_of(front, inverses, panel_of(corner, inverses, None))
+    span = n_col // groups
+    piece = lax.dynamic_slice_in_dim(factor_rows, my_col % span * col_loc, col_loc, 0)
+    spots = [(col // span * n_col + col, col) for col in range(n_col)]
+    sent = [
+        lax.ppermute(piece, ("half", "row", "col"), [(at, ((at // n_col) ^ way) * n_col + col) for at, col in spots])
+        for way in range(1, groups)
+    ]
+    factor_cols = jnp.where(my_group == my_col // span, piece, functools.reduce(jnp.add, sent))
+    row_high, row_low = split(-factor_rows)
+    col_high, col_low = split(factor_cols)
+    left = jnp.concatenate([row_high, row_high, row_low], axis=1)
+    above = jnp.concatenate([col_high, col_low, col_high], axis=1)
+
+    first_sum = place(parent_front, [over], row_tab, over_tab, gates=4)
+    updated = place(first_sum, landed, row_tab, col_tab, factor=(left, above))
+    return updated, factor_rows.astype(jnp.bfloat16)
+
+
+def general(parent_front, child_blocks, row_maps, inverse_blocks):
     row_loc, col_loc = parent_front.shape
     child_rows, child_cols = (child_blocks.shape[1], child_blocks.shape[2])
     n_row = lax.axis_size("row")
@@ -86,14 +413,15 @@
         outgoing, ("half", "row"), split_axis=0, concat_axis=0, tiled=True
     ).reshape(2, slab_rows, n_col * cap_cols)
     row_dest = row_table.reshape(2, slab_rows)
-    assembled = parent_front
+    extra = jnp.zeros_like(parent_front)
     for child in range(2):
         spread = (
             jnp.zeros((slab_rows, col_loc), jnp.float32)
             .at[:, col_table[child]]
             .add(landed[child], mode="drop")
         )
-        assembled = assembled.at[row_dest[child]].add(spread, mode="drop")
+        extra = extra.at[row_dest[child]].add(spread, mode="drop")
+    assembled = parent_front + extra
     width = inverse_blocks.shape[1]
     count = inverse_blocks.shape[0]
     span = n_col // groups
@@ -125,6 +453,20 @@
     return (updated_front, factor_rows.astype(jnp.bfloat16))
 
 
+def local(parent_front, child_blocks, row_maps, inverse_blocks):
+    col_loc = parent_front.shape[1]
+    n_col = lax.axis_size("col")
+    n_row = lax.axis_size("row")
+    groups = lax.axis_size("half") * n_row
+    share = child_blocks.shape[2] // n_col
+    panel = inverse_blocks.shape[0] * inverse_blocks.shape[1]
+    args = (parent_front, child_blocks, row_maps, inverse_blocks)
+    if share % LANES or groups & (groups - 1) or panel > min(parent_front.shape):
+        return general(*args)
+    plan = column_plan(row_maps, col_loc, n_col, share, panel)
+    return lax.cond(plan[-1] <= share, lambda *given: even(*given, plan), general, *args)
+
+
 def solution(mesh):
     in_specs = (P(("half", "row"), "col"), P("half", "row", "col"), P(), P())
     out_specs = (P(("half", "row"), "col"), P(("half", "row"), None))

time: 2420 us -> 2330 us (0.963)
  Pallas kernels: 0 us -> 1280 us
  waiting for transfers between devices: 1570 us -> 611 us
  local copies, waits for them, and re-layouts: 421 us -> 148 us
  other arithmetic: 281 us -> 68.3 us
  loops' own time: 0 us -> 48.4 us
  starting transfers between devices: 21.1 us -> 51.1 us
    pallas_call x0 -> x8, Pallas kernels: none -> 1280 us  [the longest x5 983 us: windows(): pl.pallas_call(functools.partial(window_kernel, count), in_specs=[pl.Bloc...]
    all_to_all x2 -> x4, waiting for transfers between devices: 1140 us -> 292 us  [even(): lax.all_to_all(packed(pairs[chunk], pick), 'col', split_axis=0, concat_ax...]
    psum x5 -> x1, waiting for transfers between devices: 434 us -> 162 us  [even(): front = lax.psum(front, 'col')]
    scatter-add x4 -> x0, other arithmetic: 218 us -> none  [the longest x2 124 us: local(): assembled = assembled.at[row_dest[child]].add(spread, mode='drop')]
    ppermute x0 -> x21, waiting for transfers between devices: none -> 157 us  [the longest x15 156 us: row_exchange(): lax.ppermute(pieces[way], ('half', 'row'), swaps[way])]
    scatter x3 -> x0, local copies, waits for them, and re-layouts: 141 us -> none  [the longest x1 60.5 us: row_tables(): table = jnp.full((groups * cap_rows,), row_loc, jnp.int32).at[where_at.re...]
    unnamed x40 -> x7, local copies, waits for them, and re-layouts: 93.8 us -> 23 us
    slice x8 -> x15, local copies, waits for them, and re-layouts: 83 us -> 13.6 us  [the longest x4 6.95 us: table(): rows[chunk]]
  transfers between devices with their start and end apart: 7 -> 27, of which waited for: 7 -> 10; matrix products, arithmetic and copies ran while one was open for 6% -> 8% of each run, Pallas kernels for 0% -> 39%
where the time goes in v2:
time: 2330 us; the launch traced here: 2320 us
  Pallas kernels  1280 us (55%)
  waiting for transfers between devices  611 us (26%)
  local copies, waits for them, and re-layouts  148 us (6%)
  matrix products  99.2 us (4%)
  other arithmetic  68.3 us (3%)
  starting transfers between devices  51.1 us (2%)
  loops' own time  48.4 us (2%)
    pallas_call x5, Pallas kernels, windows(): pl.pallas_call(functools.partial(window_kernel, count), in_specs=[pl.Bloc...  983 us
    pallas_call x3, Pallas kernels, place(): pl.pallas_call(functools.partial(place_kernel, (parts, n_src, n_col, gate...  297 us
    all_to_all x4, waiting for transfers between devices, even(): lax.all_to_all(packed(pairs[chunk], pick), 'col', split_axis=0, concat_ax...  292 us
    psum x1, waiting for transfers between devices, even(): front = lax.psum(front, 'col')  162 us
    ppermute x15, waiting for transfers between devices, row_exchange(): lax.ppermute(pieces[way], ('half', 'row'), swaps[way])  156 us
    gather x4, local copies, waits for them, and re-layouts, even(): pairs = [split(mine[from_row[chunk::CHUNKS]]) for chunk in range(CHUNKS)]  49.1 us
    unnamed x1, loops' own time  48.4 us
  transfers between devices with their start and end apart: 27, of which 10 were waited for; matrix products, arithmetic and copies ran while one was open for 8% of the time, Pallas kernels for 39%

profile of v2, /device:TPU:0, one launch (start us, length us, event | category | flops | bytes accessed | tf_op | source)
XLA Modules:
  0.0 2320.4 jit_solution(9770162483438527637)
XLA Ops:
  7.2 23.0 copy.348
  34.3 2279.2 %conditional.2 = (f32[4096,2048]{1,0:T(8,128)}, bf16[4096,512]{1,0:T(8,128)(2,1)}) conditional(s32[]{:T(128)} %convert_element_type.102, (s32[2,8192]{1,0:T(2,128)S(1)}, f32[1,4096,1024]{2,1,0:T(8,128)}, f32[4096,2048]{1,0:T(8,128)}, f32[4,128,128]{2,1,0:T(8,128)S(1)}) %tuple.132, (s32[2,8192]{1,0:T(2,128)S(1)}, s32[2,8,1024]{2,1,0:T(8,128)S(1)}, ...), branch_computations={%region_3.23_spmd, %region_23.37_spmd} | conditional | flops 169911336960 | bytes 1291480704
  91.7 7.8 slice_select_fusion.base
  112.1 12.2 gather_fusion.1
  128.5 12.2 gather_fusion.3
  144.9 12.2 gather_fusion.2
  161.4 12.5 gather_fusion.4
  180.3 196.6 %windows.5 = (f32[8,392,128]{2,1,0:T(8,128)}, f32[8,392,128]{2,1,0:T(8,128)}, f32[8,392,128]{2,1,0:T(8,128)}, f32[8,392,128]{2,1,0:T(8,128)}) custom-call(s32[32]{0:T(128)} %reshape.996.starts, f32[8,1024,128]{2,1,0:T(8,128)} %pad_maximum_fusion.3.values), custom_call_target="tpu_custom_call" | custom-call | bytes 12845056 | tf_op jit(solution)/shard_map/cond/branch_1_fun/windows/pallas_call | solution.py:104
  407.2 9.0 collective-permute-done
  420.9 28.1 %collective-permute-done.2 = f32[8,392,128]{2,1,0:T(8,128)} collective-permute-done((f32[8,392,128]{2,1,0:T(8,128)}, f32[8,392,128]{2,1,0:T(8,128)}, u32[]{:S(2)}, u32[]{:S(2)}) %collective-permute-start.2) | collective-permute-done | bytes 1605664 | tf_op jit(solution)/shard_map/cond/branch_1_fun/ppermute | solution.py:343
  451.7 28.4 %place.4 = f32[4096,512]{1,0:T(8,128)} custom-call(s32[256]{0:T(256)} %reshape.991.starts, s32[32]{0:T(128)} %reshape.992.rounds, s32[1]{0:T(128)} %constant.559.clone.flags, s32[16,392,1]{2,1,0:T(8,128)} %and_select_fusion.row_tab, s32[256,1]{1,0:T(8,128)} %copy.216.col_tab, f32[4096,512]{1,0:T(8,128)} %slice_select_fusion.base, ...), custom_call_target="tpu_custom_call" | custom-call | flops 2147483648 | bytes 19988480 | tf_op jit(solution)/shard_map/cond/branch_1_fun/place/pallas_call | solution.py:240
  493.3 6.0 all-to-all-start.5
  508.0 161.9 %all-to-all-done.5.values = f32[8,1024,128]{2,1,0:T(8,128)} async-done(((f32[8,1024,128]{2,1,0:T(8,128)}), f32[8,1024,128]{2,1,0:T(8,128)}, u32[]{:S(2)}, u32[]{:S(2)}) %all-to-all-start.5) | async-done | bytes 4194336 | tf_op jit(solution)/shard_map/cond/branch_1_fun/all_to_all | solution.py:367
  682.9 129.7 %all-to-all-done.3.values = f32[8,1024,128]{2,1,0:T(8,128)} async-done(((f32[8,1024,128]{2,1,0:T(8,128)}), f32[8,1024,128]{2,1,0:T(8,128)}, u32[]{:S(2)}, u32[]{:S(2)}) %all-to-all-start.3) | async-done | bytes 4194336 | tf_op jit(solution)/shard_map/cond/branch_1_fun/all_to_all | solution.py:367
  817.3 6.2 fusion.12
  823.4 161.9 %all-reduce.17.cloned.1.call-done = f32[4096,512]{1,0:T(8,128)} async-done(((f32[4096,512]{1,0:T(8,128)}), f32[4096,512]{1,0:T(8,128)}) %all-reduce.17.cloned.1.call-update) | async-done | bytes 8388624 | tf_op jit(solution)/shard_map/cond/branch_1_fun/psum | solution.py:362
  996.3 6.8 add_bitcast_fusion.3
  1032.4 9.2 convolution_subtract_fusion
  1050.2 12.9 fusion.25
  1089.0 10.4 select_reduce_fusion
  1103.6 196.6 %windows.9 = (f32[8,392,128]{2,1,0:T(8,128)}, f32[8,392,128]{2,1,0:T(8,128)}, f32[8,392,128]{2,1,0:T(8,128)}, f32[8,392,128]{2,1,0:T(8,128)}) custom-call(s32[32]{0:T(128)} %reshape.1004.starts, f32[8,1024,128]{2,1,0:T(8,128)} %all-to-all-done.5.values), custom_call_target="tpu_custom_call" | custom-call | bytes 12845056 | tf_op jit(solution)/shard_map/cond/branch_1_fun/windows/pallas_call | solution.py:104
  1300.4 196.6 %windows.7 = (f32[8,392,128]{2,1,0:T(8,128)}, f32[8,392,128]{2,1,0:T(8,128)}, f32[8,392,128]{2,1,0:T(8,128)}, f32[8,392,128]{2,1,0:T(8,128)}) custom-call(s32[32]{0:T(128)} %reshape.1002.starts, f32[8,1024,128]{2,1,0:T(8,128)} %all-to-all-done.3.values), custom_call_target="tpu_custom_call" | custom-call | bytes 12845056 | tf_op jit(solution)/shard_map/cond/branch_1_fun/windows/pallas_call | solution.py:104
  1497.0 196.6 %windows.8 = (f32[8,392,128]{2,1,0:T(8,128)}, f32[8,392,128]{2,1,0:T(8,128)}, f32[8,392,128]{2,1,0:T(8,128)}, f32[8,392,128]{2,1,0:T(8,128)}) custom-call(s32[32]{0:T(128)} %reshape.1003.starts, f32[8,1024,128]{2,1,0:T(8,128)} %all-to-all-done.4.values), custom_call_target="tpu_custom_call" | custom-call | bytes 12845056 | tf_op jit(solution)/shard_map/cond/branch_1_fun/windows/pallas_call | solution.py:104
  1693.6 196.6 %windows.6 = (f32[8,392,128]{2,1,0:T(8,128)}, f32[8,392,128]{2,1,0:T(8,128)}, f32[8,392,128]{2,1,0:T(8,128)}, f32[8,392,128]{2,1,0:T(8,128)}) custom-call(s32[32]{0:T(128)} %reshape.1001.starts, f32[8,1024,128]{2,1,0:T(8,128)} %all-to-all-done.2.values), custom_call_target="tpu_custom_call" | custom-call | bytes 12845056 | tf_op jit(solution)/shard_map/cond/branch_1_fun/windows/pallas_call | solution.py:104
  1897.1 5.8 pad_maximum_fusion.refs_16_
  1907.3 9.7 fusion.32
  1922.8 18.0 collective-permute-done.14.refs_15_
  1941.1 34.6 %collective-permute-done.6.refs_5_ = f32[8,392,128]{2,1,0:T(8,128)} collective-permute-done((f32[8,392,128]{2,1,0:T(8,128)}, f32[8,392,128]{2,1,0:T(8,128)}, u32[]{:S(2)}, u32[]{:S(2)}) %collective-permute-start.6) | collective-permute-done | bytes 1605664 | tf_op jit(solution)/shard_map/cond/branch_1_fun/ppermute | solution.py:343
  1977.8 31.8 %collective-permute-done.8.refs_7_ = f32[8,392,128]{2,1,0:T(8,128)} collective-permute-done((f32[8,392,128]{2,1,0:T(8,128)}, f32[8,392,128]{2,1,0:T(8,128)}, u32[]{:S(2)}, u32[]{:S(2)}) %collective-permute-start.8) | collective-permute-done | bytes 1605664 | tf_op jit(solution)/shard_map/cond/branch_1_fun/ppermute | solution.py:343
  2009.9 34.6 %collective-permute-done.9.refs_9_ = f32[8,392,128]{2,1,0:T(8,128)} collective-permute-done((f32[8,392,128]{2,1,0:T(8,128)}, f32[8,392,128]{2,1,0:T(8,128)}, u32[]{:S(2)}, u32[]{:S(2)}) %collective-permute-start.9) | collective-permute-done | bytes 1605664 | tf_op jit(solution)/shard_map/cond/branch_1_fun/ppermute | solution.py:343
  2044.9 109.4 %place.3.base = f32[4096,2048]{1,0:T(8,128)} custom-call(s32[256]{0:T(256)} %reshape.991.starts, s32[32]{0:T(128)} %reshape.994.rounds, s32[4]{0:T(128)} %copy-done.45, s32[16,392,1]{2,1,0:T(8,128)} %and_select_fusion.row_tab, s32[2048,1]{1,0:T(8,128)} %copy.203.col_tab, f32[4096,2048]{1,0:T(8,128)} %get-tuple-element.81.base, f32[8,4,4,392,128]{4,3,2,1,0:T(8,128)} %bitcast.484), custom_call_target="tpu_custom_call" | custom-call | flops 68719476736 | bytes 92798976 | tf_op jit(solution)/shard_map/cond/branch_1_fun/place/pallas_call | solution.py:240
  2154.4 158.9 %place.5 = f32[4096,2048]{1,0:T(8,128)} custom-call(s32[256]{0:T(256)} %reshape.991.starts, s32[32]{0:T(128)} %reshape.992.rounds, s32[1]{0:T(128)} %constant.559.clone.flags, s32[16,392,1]{2,1,0:T(8,128)} %and_select_fusion.row_tab, s32[2048,1]{1,0:T(8,128)} %copy.221.col_tab, f32[4096,2048]{1,0:T(8,128)} %place.3.base, ...), custom_call_target="tpu_custom_call" | custom-call | flops 68719476736 | bytes 92798976 | tf_op jit(solution)/shard_map/cond/branch_1_fun/place/pallas_call | solution.py:240
  (288 shorter events, 221.0 us)
Async XLA Ops:
  43.4 56.1 %copy-start.19 = (s32[2,8192]{1,0:T(2,128)}, s32[2,8192]{1,0:T(2,128)S(1)}, u32[]{:S(2)}) copy-start(s32[2,8192]{1,0:T(2,128)S(1)} %get-tuple-element.72) | copy-start | bytes 196612 | tf_op jit(solution)/shard_map/conditional
  43.4 56.1 %copy-start.26 = (f32[4,128,128]{2,1,0:T(8,128)}, f32[4,128,128]{2,1,0:T(8,128)S(1)}, u32[]{:S(2)}) copy-start(f32[4,128,128]{2,1,0:T(8,128)S(1)} %get-tuple-element.103) | copy-start | bytes 786436 | tf_op jit(solution)/shard_map/conditional
  43.5 56.7 %sort.9.cloned.1.call-start = ((), (), s32[]{:S(2)}) async-start(), calls=%async_computation.13 | async-start | bytes 196640 | tf_op jit(solution)/shard_map/cond/branch_1_fun/jit(sort)/sort | solution.py:320
  44.8 940.6 %all-reduce.17.cloned.1.call-start = ((), (), s32[]{:S(2)}) async-start(), calls=%async_computation.11 | async-start | bytes 16777216 | tf_op jit(solution)/shard_map/cond/branch_1_fun/psum | solution.py:362
  376.9 39.2 %collective-permute-start = (f32[8,392,128]{2,1,0:T(8,128)}, f32[8,392,128]{2,1,0:T(8,128)}, u32[]{:S(2)}, u32[]{:S(2)}) collective-permute-start(f32[8,392,128]{2,1,0:T(8,128)} %get-tuple-element.84), channel_id=1, source_target_pairs={{0,8},{8,0},{16,24},{24,16},{1,9},{9,1},{17,25},{25,17},{2,10},{10... | collective-permute-start | bytes 4816904 | tf_op jit(solution)/shard_map/cond/branch_1_fun/ppermute | solution.py:343
  379.9 38.6 %collective-permute-start.1 = (f32[8,392,128]{2,1,0:T(8,128)}, f32[8,392,128]{2,1,0:T(8,128)}, u32[]{:S(2)}, u32[]{:S(2)}) collective-permute-start(f32[8,392,128]{2,1,0:T(8,128)} %get-tuple-element.85), channel_id=1, source_target_pairs={{0,16},{8,24},{16,0},{24,8},{1,17},{9,25},{17,1},{25,9},{2,18},{10... | collective-permute-start | bytes 4816904 | tf_op jit(solution)/shard_map/cond/branch_1_fun/ppermute | solution.py:343
  398.3 50.7 %collective-permute-start.2 = (f32[8,392,128]{2,1,0:T(8,128)}, f32[8,392,128]{2,1,0:T(8,128)}, u32[]{:S(2)}, u32[]{:S(2)}) collective-permute-start(f32[8,392,128]{2,1,0:T(8,128)} %get-tuple-element.86), channel_id=1, source_target_pairs={{0,24},{8,16},{16,8},{24,0},{1,25},{9,17},{17,9},{25,1},{2,26},{10... | collective-permute-start | bytes 4816904 | tf_op jit(solution)/shard_map/cond/branch_1_fun/ppermute | solution.py:343
  480.2 1564.7 %all-gather.3.cloned.1.call-start = ((), (), s32[]{:S(2)}) async-start(), calls=%async_computation.12 | async-start | bytes 28901376 | tf_op jit(solution)/shard_map/cond/branch_1_fun/all_gather | solution.py:363
  493.3 176.5 %all-to-all-start.5 = ((f32[8,1024,128]{2,1,0:T(8,128)}), f32[8,1024,128]{2,1,0:T(8,128)}, u32[]{:S(2)}, u32[]{:S(2)}) async-start(f32[8,1024,128]{2,1,0:T(8,128)} %add_bitcast_fusion), calls=%async_computation.5 | async-start | bytes 8388608 | tf_op jit(solution)/shard_map/cond/branch_1_fun/all_to_all | solution.py:367
  669.9 142.8 %all-to-all-start.3 = ((f32[8,1024,128]{2,1,0:T(8,128)}), f32[8,1024,128]{2,1,0:T(8,128)}, u32[]{:S(2)}, u32[]{:S(2)}) async-start(f32[8,1024,128]{2,1,0:T(8,128)} %add_bitcast_fusion.2), calls=%async_computation.3 | async-start | bytes 8388608 | tf_op jit(solution)/shard_map/cond/branch_1_fun/all_to_all | solution.py:367
  682.9 134.3 %copy-start.27 = (f32[4,128,128]{2,1,0:T(8,128)S(1)}, f32[4,128,128]{2,1,0:T(8,128)}, u32[]{:S(2)}) copy-start(f32[4,128,128]{2,1,0:T(8,128)} %copy-done.26) | copy-start | bytes 786436 | tf_op jit(solution)/shard_map/conditional
  812.6 190.5 %all-to-all-start.4 = ((f32[8,1024,128]{2,1,0:T(8,128)}), f32[8,1024,128]{2,1,0:T(8,128)}, u32[]{:S(2)}, u32[]{:S(2)}) async-start(f32[8,1024,128]{2,1,0:T(8,128)} %add_bitcast_fusion.1), calls=%async_computation.4 | async-start | bytes 8388608 | tf_op jit(solution)/shard_map/cond/branch_1_fun/all_to_all | solution.py:367
  987.6 25.7 %collective-permute-start.17 = (f32[512,512]{1,0:T(8,128)}, f32[512,512]{1,0:T(8,128)}, u32[]{:S(2)}, u32[]{:S(2)}) collective-permute-start(f32[512,512]{1,0:T(8,128)} %slice.409), channel_id=1, source_target_pairs={{0,24},{1,25},{2,26},{3,27},{4,28},{5,29},{6,30},{7,31}} | collective-permute-start | bytes 3145736 | tf_op jit(solution)/shard_map/cond/branch_1_fun/ppermute | solution.py:372
  991.7 21.7 collective-permute-start.16
  994.0 20.6 collective-permute-start.15
  1003.1 690.5 %all-to-all-start.2 = ((f32[8,1024,128]{2,1,0:T(8,128)}), f32[8,1024,128]{2,1,0:T(8,128)}, u32[]{:S(2)}, u32[]{:S(2)}) async-start(f32[8,1024,128]{2,1,0:T(8,128)} %add_bitcast_fusion.3), calls=%async_computation.2 | async-start | bytes 8388608 | tf_op jit(solution)/shard_map/cond/branch_1_fun/all_to_all | solution.py:367
  1074.2 830.9 %collective-permute-start.20 = (f32[2048,512]{1,0:T(8,128)}, f32[2048,512]{1,0:T(8,128)}, u32[]{:S(2)}, u32[]{:S(2)}) collective-permute-start(f32[2048,512]{1,0:T(8,128)} %constant_dynamic-slice_fusion), channel_id=1, source_target_pairs={{0,24},{1,25},{10,18},{11,19},{20,12},{21,13},{30,6},{31,7}} | collective-permute-start | bytes 12582920 | tf_op jit(solution)/shard_map/cond/branch_1_fun/ppermute | solution.py:380
  1077.5 827.7 %collective-permute-start.19 = (f32[2048,512]{1,0:T(8,128)}, f32[2048,512]{1,0:T(8,128)}, u32[]{:S(2)}, u32[]{:S(2)}) collective-permute-start(f32[2048,512]{1,0:T(8,128)} %constant_dynamic-slice_fusion), channel_id=1, source_target_pairs={{0,16},{1,17},{10,26},{11,27},{20,4},{21,5},{30,14},{31,15}} | collective-permute-start | bytes 12582920 | tf_op jit(solution)/shard_map/cond/branch_1_fun/ppermute | solution.py:380
  1080.7 826.4 %collective-permute-start.18 = (f32[2048,512]{1,0:T(8,128)}, f32[2048,512]{1,0:T(8,128)}, u32[]{:S(2)}, u32[]{:S(2)}) collective-permute-start(f32[2048,512]{1,0:T(8,128)} %constant_dynamic-slice_fusion), channel_id=1, source_target_pairs={{0,8},{1,9},{10,2},{11,3},{20,28},{21,29},{30,22},{31,23}} | collective-permute-start | bytes 12582920 | tf_op jit(solution)/shard_map/cond/branch_1_fun/ppermute | solution.py:380
  1099.8 397.2 %copy-start.45 = (s32[4]{0:T(128)}, s32[4]{0:T(128)S(1)}, u32[]{:S(2)}) copy-start(s32[4]{0:T(128)S(1)} %convert_element_type.106.flags) | copy-start | bytes 52 | tf_op jit(solution)/shard_map/conditional
  1300.2 602.8 %collective-permute-start.12 = (f32[8,392,128]{2,1,0:T(8,128)}, f32[8,392,128]{2,1,0:T(8,128)}, u32[]{:S(2)}, u32[]{:S(2)}) collective-permute-start(f32[8,392,128]{2,1,0:T(8,128)} %get-tuple-element.100), channel_id=1, source_target_pairs={{0,8},{8,0},{16,24},{24,16},{1,9},{9,1},{17,25},{25,17},{2,10},{10... | collective-permute-start | bytes 4816904 | tf_op jit(solution)/shard_map/cond/branch_1_fun/ppermute | solution.py:343
  1300.3 604.7 %collective-permute-start.13 = (f32[8,392,128]{2,1,0:T(8,128)}, f32[8,392,128]{2,1,0:T(8,128)}, u32[]{:S(2)}, u32[]{:S(2)}) collective-permute-start(f32[8,392,128]{2,1,0:T(8,128)} %get-tuple-element.101), channel_id=1, source_target_pairs={{0,16},{8,24},{16,0},{24,8},{1,17},{9,25},{17,1},{25,9},{2,18},{10... | collective-permute-start | bytes 4816904 | tf_op jit(solution)/shard_map/cond/branch_1_fun/ppermute | solution.py:343
  1903.0 37.8 %collective-permute-start.14 = (f32[8,392,128]{2,1,0:T(8,128)}, f32[8,392,128]{2,1,0:T(8,128)}, u32[]{:S(2)}, u32[]{:S(2)}) collective-permute-start(f32[8,392,128]{2,1,0:T(8,128)} %get-tuple-element.102), channel_id=1, source_target_pairs={{0,24},{8,16},{16,8},{24,0},{1,25},{9,17},{17,9},{25,1},{2,26},{10... | collective-permute-start | bytes 4816904 | tf_op jit(solution)/shard_map/cond/branch_1_fun/ppermute | solution.py:343
  1905.0 70.7 %collective-permute-start.6 = (f32[8,392,128]{2,1,0:T(8,128)}, f32[8,392,128]{2,1,0:T(8,128)}, u32[]{:S(2)}, u32[]{:S(2)}) collective-permute-start(f32[8,392,128]{2,1,0:T(8,128)} %get-tuple-element.92), channel_id=1, source_target_pairs={{0,8},{8,0},{16,24},{24,16},{1,9},{9,1},{17,25},{25,17},{2,10},{10... | collective-permute-start | bytes 4816904 | tf_op jit(solution)/shard_map/cond/branch_1_fun/ppermute | solution.py:343
  1905.1 71.0 %collective-permute-start.7 = (f32[8,392,128]{2,1,0:T(8,128)}, f32[8,392,128]{2,1,0:T(8,128)}, u32[]{:S(2)}, u32[]{:S(2)}) collective-permute-start(f32[8,392,128]{2,1,0:T(8,128)} %get-tuple-element.93), channel_id=1, source_target_pairs={{0,16},{8,24},{16,0},{24,8},{1,17},{9,25},{17,1},{25,9},{2,18},{10... | collective-permute-start | bytes 4816904 | tf_op jit(solution)/shard_map/cond/branch_1_fun/ppermute | solution.py:343
  1905.2 104.4 %collective-permute-start.8 = (f32[8,392,128]{2,1,0:T(8,128)}, f32[8,392,128]{2,1,0:T(8,128)}, u32[]{:S(2)}, u32[]{:S(2)}) collective-permute-start(f32[8,392,128]{2,1,0:T(8,128)} %get-tuple-element.94), channel_id=1, source_target_pairs={{0,24},{8,16},{16,8},{24,0},{1,25},{9,17},{17,9},{25,1},{2,26},{10... | collective-permute-start | bytes 4816904 | tf_op jit(solution)/shard_map/cond/branch_1_fun/ppermute | solution.py:343
  1907.2 137.3 %collective-permute-start.9 = (f32[8,392,128]{2,1,0:T(8,128)}, f32[8,392,128]{2,1,0:T(8,128)}, u32[]{:S(2)}, u32[]{:S(2)}) collective-permute-start(f32[8,392,128]{2,1,0:T(8,128)} %get-tuple-element.96), channel_id=1, source_target_pairs={{0,8},{8,0},{16,24},{24,16},{1,9},{9,1},{17,25},{25,17},{2,10},{10... | collective-permute-start | bytes 4816904 | tf_op jit(solution)/shard_map/cond/branch_1_fun/ppermute | solution.py:343
  1940.8 213.6 %collective-permute-start.10 = (f32[8,392,128]{2,1,0:T(8,128)}, f32[8,392,128]{2,1,0:T(8,128)}, u32[]{:S(2)}, u32[]{:S(2)}) collective-permute-start(f32[8,392,128]{2,1,0:T(8,128)} %get-tuple-element.97), channel_id=1, source_target_pairs={{0,16},{8,24},{16,0},{24,8},{1,17},{9,25},{17,1},{25,9},{2,18},{10... | collective-permute-start | bytes 4816904 | tf_op jit(solution)/shard_map/cond/branch_1_fun/ppermute | solution.py:343
  1975.7 178.7 %collective-permute-start.11 = (f32[8,392,128]{2,1,0:T(8,128)S(1)}, f32[8,392,128]{2,1,0:T(8,128)}, u32[]{:S(2)}, u32[]{:S(2)}) collective-permute-start(f32[8,392,128]{2,1,0:T(8,128)S(1)} %copy-done.44), channel_id=1, source_target_pairs={{0,24},{8,16},{16,8},{24,0},{1,25},{9,17},{17,9},{25,1},{2,26},{10... | collective-permute-start | bytes 4816904 | tf_op jit(solution)/shard_map/cond/branch_1_fun/ppermute | solution.py:343
  1976.1 178.3 %collective-permute-start.3 = (f32[8,392,128]{2,1,0:T(8,128)}, f32[8,392,128]{2,1,0:T(8,128)}, u32[]{:S(2)}, u32[]{:S(2)}) collective-permute-start(f32[8,392,128]{2,1,0:T(8,128)} %get-tuple-element.88), channel_id=1, source_target_pairs={{0,8},{8,0},{16,24},{24,16},{1,9},{9,1},{17,25},{25,17},{2,10},{10... | collective-permute-start | bytes 4816904 | tf_op jit(solution)/shard_map/cond/branch_1_fun/ppermute | solution.py:343
  2009.6 144.8 %collective-permute-start.4 = (f32[8,392,128]{2,1,0:T(8,128)}, f32[8,392,128]{2,1,0:T(8,128)}, u32[]{:S(2)}, u32[]{:S(2)}) collective-permute-start(f32[8,392,128]{2,1,0:T(8,128)} %get-tuple-element.89), channel_id=1, source_target_pairs={{0,16},{8,24},{16,0},{24,8},{1,17},{9,25},{17,1},{25,9},{2,18},{10... | collective-permute-start | bytes 4816904 | tf_op jit(solution)/shard_map/cond/branch_1_fun/ppermute | solution.py:343
  2044.5 109.9 %collective-permute-start.5 = (f32[8,392,128]{2,1,0:T(8,128)}, f32[8,392,128]{2,1,0:T(8,128)}, u32[]{:S(2)}, u32[]{:S(2)}) collective-permute-start(f32[8,392,128]{2,1,0:T(8,128)} %get-tuple-element.90), channel_id=1, source_target_pairs={{0,24},{8,16},{16,8},{24,0},{1,25},{9,17},{17,9},{25,1},{2,26},{10... | collective-permute-start | bytes 4816904 | tf_op jit(solution)/shard_map/cond/branch_1_fun/ppermute | solution.py:343
  (35 other events, 328.8 us)
Sparse Core Ops, SparseCore 0:
  47.3 14.3 sort.11.cloned.1.call-done
  480.3 504.9 all-reduce.16
  987.0 534.2 all-gather.2
  (1 shorter events, 0.0 us)
